TPU v7x, 256 devices: a whole 4x4x8 slice. The times are simulated.
256 devices in a mesh: dp: 16 (over z, core), seq: 16 (over y, x).
Axes of the slice: x: 4, y: 4, z: 8, core: 2. Of those that a mesh axis runs over, the one named last changes fastest.
Arguments:
- tokens: bfloat16 [16, 16, 320, 1152], P('dp', 'seq'), may hold values from -6 to 6
- cotangent: bfloat16 [16, 16, 320, 1152], P('dp', 'seq'), may hold values from -6 to 6
- modulation: float32 [16, 6, 1152], P('dp'), may hold values from -3 to 3
- lengths: int32 [16], P('dp'), may hold values from 1 to 16, as said below
- w_spatial_qkv: bfloat16 [1152, 1728], replicated, may hold values from -1 to 1
- w_spatial_out: bfloat16 [576, 1152], replicated, may hold values from -0.25 to 0.25
- w_temporal_qkv: bfloat16 [1152, 1728], replicated, may hold values from -1 to 1
- w_temporal_out: bfloat16 [576, 1152], replicated, may hold values from -0.25 to 0.25
Outputs:
- grad_tokens: bfloat16 [16, 16, 320, 1152], P('dp', 'seq')
- grad_spatial_qkv: bfloat16 [1152, 1728], P('seq')
- grad_spatial_out: bfloat16 [576, 1152], P('seq')
- grad_temporal_qkv: bfloat16 [1152, 1728], P('seq')
- grad_temporal_out: bfloat16 [576, 1152], P('seq')
Inputs may be any that keep to these rules, and one draw needn't show every extreme that they name: `lengths`: frames of each clip that hold data; later frames are padding. Some clip holds all 16 frames and some other clip only its first.
All inputs are finite; a program needn't handle non-finite values.
Results may differ from a plain program's by a relative error of at most 0.04.
Values may be sent and summed in bfloat16 or wider, within the bound.
A program may use at most 192 MiB of HBM per device.

v0:
```python
import jax
import jax.numpy as jnp
from jax import lax
from jax.sharding import PartitionSpec as P

HEADS = 8
HEAD_DIM = 72
F = 16


NORM_EPS = 1e-06
MASKED = -1e30
SPATIAL_FORMS = ("cfqhd", "cfkhd", "cfhqk")
TEMPORAL_FORMS = ("cqphd", "ckphd", "cphqk")


def modulated_norm(source, shift, scale):
    average = jnp.mean(source, axis=-1, keepdims=True)
    centred = source - average
    variance = jnp.mean(centred * centred, axis=-1, keepdims=True)
    return centred * lax.rsqrt(variance + NORM_EPS) * (1.0 + scale) + shift


def norm_back(source, shift, scale, upstream):
    pullback = jax.vjp(lambda inputs: modulated_norm(inputs, shift, scale), source)[1]
    return pullback(upstream)[0]


def split_heads(packed):
    return packed.reshape(packed.shape[:-1] + (HEADS, HEAD_DIM))


def merge_heads(spread):
    return spread.reshape(spread.shape[:-2] + (HEADS * HEAD_DIM,))


def product(form_left, form_right, form_out, left_side, right_side):
    return jnp.einsum(
        form_left + "," + form_right + "->" + form_out,
        left_side,
        right_side,
        preferred_element_type=jnp.float32,
    )


def thirds(packed):
    inner_width = HEADS * HEAD_DIM
    return (
        split_heads(packed[..., :inner_width]),
        split_heads(packed[..., inner_width : 2 * inner_width]),
        split_heads(packed[..., 2 * inner_width :]),
    )


def attention_probs(query_rows, key_rows, keep, forms):
    scores = product(forms[0], forms[1], forms[2], query_rows, key_rows) * HEAD_DIM ** (-0.5)
    scores = jnp.where(keep, scores, MASKED)
    highest = jnp.max(scores, axis=-1, keepdims=True)
    exponent = jnp.exp(scores - highest)
    return exponent / jnp.sum(exponent, axis=-1, keepdims=True)


def attend_forward(packed, keep, forms):
    query_rows, key_rows, value_rows = thirds(packed)
    soft_rounded = attention_probs(query_rows, key_rows, keep, forms).astype(jnp.bfloat16)
    mixed = product(forms[2], forms[1], forms[0], soft_rounded, value_rows)
    return merge_heads(mixed).astype(jnp.bfloat16)


def attend_backward(packed, keep, upstream, forms):
    query_rows, key_rows, value_rows = thirds(packed)
    soft_weights = attention_probs(query_rows, key_rows, keep, forms)
    soft_rounded = soft_weights.astype(jnp.bfloat16)
    grad_heads = split_heads(upstream)
    grad_values = product(forms[2], forms[0], forms[1], soft_rounded, grad_heads).astype(
        jnp.bfloat16
    )
    grad_raw = product(forms[0], forms[1], forms[2], grad_heads, value_rows)
    centred = grad_raw - jnp.sum(grad_raw * soft_weights, axis=-1, keepdims=True)
    grad_scores = (soft_weights * centred * HEAD_DIM ** (-0.5)).astype(jnp.bfloat16)
    grad_queries = product(forms[2], forms[1], forms[0], grad_scores, key_rows).astype(jnp.bfloat16)
    grad_keys = product(forms[2], forms[0], forms[1], grad_scores, query_rows).astype(jnp.bfloat16)
    return jnp.concatenate(
        [merge_heads(grad_queries), merge_heads(grad_keys), merge_heads(grad_values)], axis=-1
    )


def project(rows, weight):
    flat = rows.reshape(-1, rows.shape[-1])
    result = jnp.dot(flat, weight, preferred_element_type=jnp.float32)
    return result.reshape(rows.shape[:-1] + (weight.shape[1],))


def project_back(grads, weight):
    flat = grads.reshape(-1, grads.shape[-1])
    result = lax.dot_general(
        flat, weight, (((1,), (1,)), ((), ())), preferred_element_type=jnp.float32
    )
    return result.reshape(grads.shape[:-1] + (weight.shape[0],))


def weight_grad(rows, grads):
    return lax.dot_general(
        rows.reshape(-1, rows.shape[-1]),
        grads.reshape(-1, grads.shape[-1]),
        (((0,), (0,)), ((), ())),
        preferred_element_type=jnp.float32,
    )


def guarded(function, operands):
    return function(*operands)


def reduce_grads(first_grad, second_grad, third_grad, fourth_grad):
    row_parts = (
        lax.psum_scatter(
            first_grad.astype(jnp.bfloat16), "seq", scatter_dimension=0, tiled=True
        ).astype(jnp.float32),
        lax.psum_scatter(
            second_grad.astype(jnp.bfloat16), "seq", scatter_dimension=0, tiled=True
        ).astype(jnp.float32),
        lax.psum_scatter(
            third_grad.astype(jnp.bfloat16), "seq", scatter_dimension=0, tiled=True
        ).astype(jnp.float32),
        lax.psum_scatter(
            fourth_grad.astype(jnp.bfloat16), "seq", scatter_dimension=0, tiled=True
        ).astype(jnp.float32),
    )
    summed = (
        lax.psum(row_parts[0].astype(jnp.bfloat16), "dp").astype(jnp.float32),
        lax.psum(row_parts[1].astype(jnp.bfloat16), "dp").astype(jnp.float32),
        lax.psum(row_parts[2].astype(jnp.bfloat16), "dp").astype(jnp.float32),
        lax.psum(row_parts[3].astype(jnp.bfloat16), "dp").astype(jnp.float32),
    )
    return tuple((piece.astype(jnp.bfloat16) for piece in summed))


def local(
    tokens,
    cotangent,
    modulation,
    lengths,
    w_spatial_qkv,
    w_spatial_out,
    w_temporal_qkv,
    w_temporal_out,
):
    frames_here = tokens.shape[1]
    position = lax.axis_index("seq") * frames_here + jnp.arange(frames_here, dtype=jnp.int32)
    live = (position[None, :] < lengths[:, None]).astype(jnp.float32)
    factors = modulation[:, :, None, None, :]
    masked = cotangent.astype(jnp.float32) * live[:, :, None, None]
    keep_time = (jnp.arange(F, dtype=jnp.int32)[None, :] < lengths[:, None])[:, None, None, None, :]

    def front(source):
        source_wide = source.astype(jnp.float32)
        normed = modulated_norm(source_wide, factors[:, 0], factors[:, 1]).astype(jnp.bfloat16)
        packed = project(normed, w_spatial_qkv).astype(jnp.bfloat16)
        mixed = attend_forward(packed, True, SPATIAL_FORMS)
        residual = (source_wide + factors[:, 2] * project(mixed, w_spatial_out)).astype(
            jnp.bfloat16
        )
        normed_time = modulated_norm(
            residual.astype(jnp.float32), factors[:, 3], factors[:, 4]
        ).astype(jnp.bfloat16)
        packed_time = project(normed_time, w_temporal_qkv).astype(jnp.bfloat16)
        return (normed, packed, mixed, residual, normed_time, packed_time)

    normed, packed, mixed, residual, normed_time, packed_time = guarded(front, (tokens,))
    by_position = lax.all_to_all(packed_time, "seq", split_axis=2, concat_axis=1, tiled=True)
    attended = attend_forward(by_position, keep_time, TEMPORAL_FORMS)
    attended_home = lax.all_to_all(attended, "seq", split_axis=1, concat_axis=2, tiled=True)

    def back_top(attended_rows, cot_rows):
        scaled_cot = (factors[:, 5] * cot_rows).astype(jnp.bfloat16)
        return (
            weight_grad(attended_rows, scaled_cot),
            project_back(scaled_cot, w_temporal_out).astype(jnp.bfloat16),
        )

    temporal_out_part, grad_attended = guarded(back_top, (attended_home, masked))
    grad_position = lax.all_to_all(grad_attended, "seq", split_axis=2, concat_axis=1, tiled=True)
    grad_packed_position = attend_backward(by_position, keep_time, grad_position, TEMPORAL_FORMS)
    grad_packed_time = lax.all_to_all(
        grad_packed_position, "seq", split_axis=1, concat_axis=2, tiled=True
    )

    def back_bottom(
        source,
        normed_rows,
        packed_rows,
        mixed_rows,
        residual_rows,
        normed_time_rows,
        grad_time_rows,
        cot_rows,
    ):
        temporal_qkv_grad = weight_grad(normed_time_rows, grad_time_rows)
        grad_residual = cot_rows + norm_back(
            residual_rows.astype(jnp.float32),
            factors[:, 3],
            factors[:, 4],
            project_back(grad_time_rows, w_temporal_qkv),
        )
        scaled_residual = (factors[:, 2] * grad_residual).astype(jnp.bfloat16)
        spatial_out_grad = weight_grad(mixed_rows, scaled_residual)
        grad_mixed = project_back(scaled_residual, w_spatial_out).astype(jnp.bfloat16)
        grad_packed = attend_backward(packed_rows, True, grad_mixed, SPATIAL_FORMS)
        spatial_qkv_grad = weight_grad(normed_rows, grad_packed)
        grad_source = grad_residual + norm_back(
            source.astype(jnp.float32),
            factors[:, 0],
            factors[:, 1],
            project_back(grad_packed, w_spatial_qkv),
        )
        return (
            grad_source.astype(jnp.bfloat16),
            spatial_qkv_grad,
            spatial_out_grad,
            temporal_qkv_grad,
        )

    grad_tokens, spatial_qkv_part, spatial_out_part, temporal_qkv_part = guarded(
        back_bottom,
        (tokens, normed, packed, mixed, residual, normed_time, grad_packed_time, masked),
    )
    summed = reduce_grads(spatial_qkv_part, spatial_out_part, temporal_qkv_part, temporal_out_part)
    return (grad_tokens, summed[0], summed[1], summed[2], summed[3])


def solution(mesh):
    placed = (
        P("dp", "seq", None, None),
        P("dp", "seq", None, None),
        P("dp", None, None),
        P("dp"),
        P(),
        P(),
        P(),
        P(),
    )
    return jax.shard_map(
        local,
        mesh=mesh,
        in_specs=placed,
        out_specs=(
            P("dp", "seq", None, None),
            P("seq", None),
            P("seq", None),
            P("seq", None),
            P("seq", None),
        ),
        check_vma=False,
    )
```

profile of v0, /device:TPU:1, one launch (start us, length us, event | category | flops | bytes accessed | tf_op | source)
XLA Modules:
  0.0 578.3 jit_solution(14811847739660207381)
XLA Ops:
  8.8 2.4 fusion.53
  12.4 3.2 reduce.37
  16.9 7.8 %all-to-all-start.1 = ((bf16[16,2,5760]{2,1,0:T(2,128)(2,1)}), bf16[16,2,5760]{2,1,0:T(2,128)(2,1)}, u32[]{:S(2)}, u32[]{:S(2)}) async-start(bf16[16,2,5760]{2,1,0:T(2,128)(2,1)} %reshape.452), calls=%async_computation.1 | async-start | bytes 737280 | tf_op jit(solution)/shard_map/all_to_all | solution.py:183
  25.9 3.9 fusion.14
  32.2 4.4 fusion.108
  36.6 2.7 convolution_convert_fusion.11
  42.1 1.8 fusion.15
  43.9 3.2 copy.153
  47.1 9.3 %reduce.36 = bf16[320,1728]{1,0:T(8,128)(2,1)S(1)} reduce(bf16[320,1,1,1728]{3,2,1,0:T(2,128)(2,1)} %bitcast.149, bf16[]{:T(256)} %broadcast.227), dimensions={1,2}, to_apply=%bitcast.145.reduce_sub_computation | reduce | bytes 2211842
  56.3 2.4 reshape.450
  58.7 6.6 %all-to-all-start = ((bf16[16,2,17280]{2,1,0:T(2,128)(2,1)}), bf16[16,2,17280]{2,1,0:T(2,128)(2,1)S(1)}, u32[]{:S(2)}, u32[]{:S(2)}) async-start(bf16[16,2,17280]{2,1,0:T(2,128)(2,1)} %reshape.450), calls=%async_computation | async-start | bytes 2211840 | tf_op jit(solution)/shard_map/all_to_all | solution.py:171
  65.4 3.6 reshape.453
  68.9 4.2 bitcast_reduce_fusion.1
  73.2 2.5 reshape.420
  75.7 5.7 all-to-all-done
  81.4 4.7 reshape.451
  86.0 9.2 %bitcast_reduce_fusion = bf16[320,1728]{1,0:T(8,128)(2,1)} fusion(bf16[320,1,1,1728]{3,2,1,0:T(2,128)(2,1)} %reshape.451), kind=kLoop, calls=%fused_computation.139 | loop fusion | bytes 2211840 | tf_op jit(solution)/shard_map/all_to_all | solution.py:171
  97.9 2.8 reshape.439
  102.9 3.4 fusion.110
  106.3 2.7 fusion.50
  110.5 2.4 reshape.434
  113.0 4.5 all-to-all-start.3
  120.5 4.1 fusion.49
  127.2 4.2 fusion.48
  133.9 2.5 concatenate.6
  137.8 6.8 %all-to-all-start.2 = ((bf16[1,16,20,1728]{3,2,0,1:T(8,128)(2,1)}), bf16[1,16,20,1728]{3,2,0,1:T(8,128)(2,1)}, u32[]{:S(2)}, u32[]{:S(2)}) async-start(bf16[1,16,20,1728]{3,2,0,1:T(8,128)(2,1)} %copy.103), calls=%async_computation.2 | async-start | bytes 2752512 | tf_op jit(solution)/shard_map/all_to_all | solution.py:185
  145.9 2.1 convolution_convert_fusion.3
  148.0 14.5 %all-to-all-done.2 = bf16[1,16,20,1728]{3,2,0,1:T(8,128)(2,1)} async-done(((bf16[1,16,20,1728]{3,2,0,1:T(8,128)(2,1)}), bf16[1,16,20,1728]{3,2,0,1:T(8,128)(2,1)}, u32[]{:S(2)}, u32[]{:S(2)}) %all-to-all-start.2) | async-done | bytes 1105952 | tf_op jit(solution)/shard_map/all_to_all | solution.py:185
  162.5 2.4 reshape.425
  164.9 4.3 fusion.35
  171.7 2.0 convolution_convert_fusion.2
  174.3 6.2 %convolution_convert_fusion = bf16[1152,1728]{1,0:T(8,128)(2,1)} fusion(bf16[320,1728]{1,0:T(8,128)(2,1)} %reshape.425, f32[1,1,320,1152]{3,2,1,0:T(8,128)} %copy-done.2, f32[1152]{0:T(1024)} %copy-done.33, f32[1152]{0:T(1024)} %copy-done.34, f32[320]{0:T(512)S(1)} %copy-done.28, f32[320]{0:T(512)S(1)} %copy-done.21), kind=kOutput, calls=%fused_computation.4 | convolution fusion | flops 1277853696 | bytes 6573568 | tf_op jit(solution)/shard_map/dot_general | solution.py:103
  180.7 2.7 convolution_convert_fusion.12
  183.4 2.0 copy.104
  185.4 3.8 fusion.115
  189.2 7.9 %fusion.42 = bf16[8,72,320]{2,1,0:T(8,128)(2,1)} fusion(bf16[320,8,72]{0,2,1:T(8,128)(2,1)} %bitcast.158, f32[8,320,320]{1,2,0:T(8,128)} %fusion.115, f32[8,320,320]{1,2,0:T(8,128)} %get-tuple-element.26, f32[8,320]{1,0:T(8,128)} %copy-done.43), kind=kOutput, calls=%fused_computation.66 | convolution fusion | flops 123886400 | bytes 7301120 | tf_op jit(solution)/shard_map/cfhqk,cfkhd->cfqhd/dot_general | solution.py:38
  197.1 8.0 %fusion.45 = bf16[8,72,320]{2,1,0:T(8,128)(2,1)} fusion(bf16[320,8,72]{0,2,1:T(8,128)(2,1)} %bitcast.155, f32[8,320,320]{1,2,0:T(8,128)} %fusion.115, f32[8,320,320]{1,2,0:T(8,128)} %get-tuple-element.26, f32[8,320]{1,0:T(8,128)} %copy-done.43), kind=kOutput, calls=%fused_computation.67 | convolution fusion | flops 123886400 | bytes 7301120 | tf_op jit(solution)/shard_map/cfhqk,cfqhd->cfkhd/dot_general | solution.py:38
  205.2 3.0 convolution_convert_fusion.10
  209.0 4.5 convolution_convert_fusion.1
  215.5 4.3 fusion.34
  222.1 57.2 %all-reduce.9.cloned.1.call-done = (bf16[576,1152]{1,0:T(8,128)(2,1)}, bf16[576,1152]{1,0:T(8,128)(2,1)}) async-done(((bf16[576,1152]{1,0:T(8,128)(2,1)}, bf16[576,1152]{1,0:T(8,128)(2,1)}), (bf16[576,1152]{1,0:T(8,128)(2,1)}, bf16[576,1152]{1,0:T(8,128)(2,1)})) %all-reduce.9.cloned.1.call-update) | async-done | bytes 2654224
  279.3 1.7 constant_dynamic-slice_fusion
  281.0 83.9 %reduce-scatter.9.cloned.1.call-done = bf16[72,1728]{1,0:T(8,128)(2,1)} async-done(((bf16[1152,1728]{1,0:T(8,128)(2,1)}), bf16[72,1728]{1,0:T(8,128)(2,1)}) %reduce-scatter.9.cloned.1.call-update) | async-done | bytes 248848
  364.9 86.4 %reduce-scatter.7.cloned.1.call-done = bf16[72,1728]{1,0:T(8,128)(2,1)} async-done(((bf16[1152,1728]{1,0:T(8,128)(2,1)}), bf16[72,1728]{1,0:T(8,128)(2,1)}) %reduce-scatter.7.cloned.1.call-update) | async-done | bytes 248848
  451.4 3.1 add_convert_fusion
  454.5 110.6 %all-reduce.11.cloned.1.call-done = (bf16[72,1728]{1,0:T(8,128)(2,1)}, bf16[36,1152]{1,0:T(8,128)(2,1)}, bf16[72,1728]{1,0:T(8,128)(2,1)}, bf16[36,1152]{1,0:T(8,128)(2,1)}) async-done(((bf16[72,1728]{1,0:T(8,128)(2,1)}, bf16[36,1152]{1,0:T(8,128)(2,1)}, bf16[72,1728]{1,0:T(8,128)(2,1)}, bf16[36,1152]{1,0:T(8,128)(2,1)}), (bf16[72,1728]{1,0:T(8,128)(2,1)}, bf16[36,1152]{1,0:T(8,128)(2,1)}, ...) | async-done | bytes 663568 | tf_op jit(solution)/shard_map/psum | solution.py:131
  565.1 1.7 copy.162
  568.3 1.7 copy.164
  (140 shorter events, 37.5 us)
Async XLA Ops:
  7.2 32.1 %copy-start = (bf16[576,1152]{1,0:T(8,128)(2,1)S(1)}, bf16[576,1152]{1,0:T(8,128)(2,1)}, u32[]{:S(2)}) copy-start(bf16[576,1152]{1,0:T(8,128)(2,1)} %param.13) | copy-start | bytes 3981316
  8.1 17.7 %copy-start.29 = (f32[1152]{0:T(1024)}, f32[1152]{0:T(1024)S(1)}, u32[]{:S(2)}) copy-start(f32[1152]{0:T(1024)S(1)} %get-tuple-element.9) | copy-start | bytes 13828
  8.1 17.7 %copy-start.31 = (f32[1152]{0:T(1024)}, f32[1152]{0:T(1024)S(1)}, u32[]{:S(2)}) copy-start(f32[1152]{0:T(1024)S(1)} %get-tuple-element.8) | copy-start | bytes 13828
  8.2 33.0 %copy-start.33 = (f32[1152]{0:T(1024)}, f32[1152]{0:T(1024)S(1)}, u32[]{:S(2)}) copy-start(f32[1152]{0:T(1024)S(1)} %get-tuple-element.6) | copy-start | bytes 13828
  8.2 33.0 %copy-start.34 = (f32[1152]{0:T(1024)}, f32[1152]{0:T(1024)S(1)}, u32[]{:S(2)}) copy-start(f32[1152]{0:T(1024)S(1)} %get-tuple-element.7) | copy-start | bytes 13828
  11.9 12.8 %copy-start.1 = (bf16[1,1,320,1152]{3,2,1,0:T(8,128)(2,1)S(1)}, bf16[1,1,320,1152]{3,2,1,0:T(8,128)(2,1)}, u32[]{:S(2)}) copy-start(bf16[1,1,320,1152]{3,2,1,0:T(8,128)(2,1)} %param.8) | copy-start | bytes 2211844
  16.9 41.9 %all-to-all-start.1 = ((bf16[16,2,5760]{2,1,0:T(2,128)(2,1)}), bf16[16,2,5760]{2,1,0:T(2,128)(2,1)}, u32[]{:S(2)}, u32[]{:S(2)}) async-start(bf16[16,2,5760]{2,1,0:T(2,128)(2,1)} %reshape.452), calls=%async_computation.1 | async-start | bytes 737280 | tf_op jit(solution)/shard_map/all_to_all | solution.py:183
  31.0 1.2 copy-start.16
  32.2 4.4 copy-start.11
  36.6 2.7 copy-start.43
  39.3 1.0 copy-start.36
  39.3 2.8 copy-start.35
  40.2 1.2 copy-start.2
  40.2 1.2 copy-start.19
  40.6 0.9 copy-start.26
  58.7 22.6 %all-to-all-start = ((bf16[16,2,17280]{2,1,0:T(2,128)(2,1)}), bf16[16,2,17280]{2,1,0:T(2,128)(2,1)S(1)}, u32[]{:S(2)}, u32[]{:S(2)}) async-start(bf16[16,2,17280]{2,1,0:T(2,128)(2,1)} %reshape.450), calls=%async_computation | async-start | bytes 2211840 | tf_op jit(solution)/shard_map/all_to_all | solution.py:171
  97.9 2.8 copy-start.10
  97.9 4.3 copy-start.9
  102.9 3.4 copy-start.8
  106.3 2.7 copy-start.42
  113.0 24.9 %all-to-all-start.3 = ((bf16[1,16,20,576]{3,2,0,1:T(8,128)(2,1)}), bf16[1,16,20,576]{3,2,0,1:T(8,128)(2,1)}, u32[]{:S(2)}, u32[]{:S(2)}) async-start(bf16[1,16,20,576]{3,2,0,1:T(8,128)(2,1)} %reshape.434), calls=%async_computation.3 | async-start | bytes 983040 | tf_op jit(solution)/shard_map/all_to_all | solution.py:173
  117.5 1.6 copy-start.15
  119.1 1.4 copy-start.14
  124.6 2.6 copy-start.13
  137.8 8.1 %copy-start.6 = (bf16[1,1,320,1152]{3,2,1,0:T(8,128)(2,1)S(1)}, bf16[1,1,320,1152]{3,2,1,0:T(8,128)(2,1)}, u32[]{:S(2)}) copy-start(bf16[1,1,320,1152]{3,2,1,0:T(8,128)(2,1)} %param.9) | copy-start | bytes 2211844
  137.8 24.7 %all-to-all-start.2 = ((bf16[1,16,20,1728]{3,2,0,1:T(8,128)(2,1)}), bf16[1,16,20,1728]{3,2,0,1:T(8,128)(2,1)}, u32[]{:S(2)}, u32[]{:S(2)}) async-start(bf16[1,16,20,1728]{3,2,0,1:T(8,128)(2,1)} %copy.103), calls=%async_computation.2 | async-start | bytes 2752512 | tf_op jit(solution)/shard_map/all_to_all | solution.py:185
  144.7 134.7 %all-reduce.9.cloned.1.call-start = ((), (), s32[]{:S(2)}) async-start(), calls=%async_computation.8 | async-start | bytes 5308416
  148.0 17.0 %copy-start.3 = (f32[1,1,320,1152]{3,2,1,0:T(8,128)S(1)}, f32[1,1,320,1152]{3,2,1,0:T(8,128)}, u32[]{:S(2)}) copy-start(f32[1,1,320,1152]{3,2,1,0:T(8,128)} %copy-done.2) | copy-start | bytes 4423684
  164.9 4.4 copy-start.25
  164.9 4.4 copy-start.4
  164.9 4.4 copy-start.20
  164.9 4.4 copy-start.27
  169.3 1.1 copy-start.7
  169.8 1.0 copy-start.17
  170.5 1.2 copy-start.37
  170.8 0.9 copy-start.12
  173.6 191.3 %reduce-scatter.9.cloned.1.call-start = ((), (), s32[]{:S(2)}) async-start(), calls=%async_computation.7 | async-start | bytes 4386816
  180.4 270.9 %reduce-scatter.7.cloned.1.call-start = ((), (), s32[]{:S(2)}) async-start(), calls=%async_computation.6 | async-start | bytes 4386816
  205.2 3.8 copy-start.30
  205.2 3.8 copy-start.32
  205.2 3.8 copy-start.38
  205.2 3.8 copy-start.39
  208.2 0.8 copy-start.40
  213.5 0.7 copy-start.41
  213.6 351.5 %all-reduce.11.cloned.1.call-start = ((), (), s32[]{:S(2)}) async-start(), calls=%async_computation.9 | async-start | bytes 1400832 | tf_op jit(solution)/shard_map/psum | solution.py:131
  215.5 4.3 copy-start.23
  219.8 1.2 copy-start.5
  221.0 230.4 %copy-start.18 = (f32[320]{0:T(512)S(1)}, f32[320]{0:T(512)}, u32[]{:S(2)}) copy-start(f32[320]{0:T(512)} %copy-done.17) | copy-start | bytes 3844
  (4 other events, 2.5 us)
Sparse Core Ops, SparseCore 0:
  173.8 105.5 all-reduce.8
  283.5 81.4 reduce-scatter.8
  368.6 82.6 reduce-scatter.6
  454.5 110.5 all-reduce.10
where the time goes:
time: 584 us; the launch traced here: 578 us
  waiting for transfers between devices  358 us (61%)
  matrix products  81.4 us (14%)
  local copies, waits for them, and re-layouts  77 us (13%)
  starting transfers between devices  26.1 us (4%)
  other arithmetic  19.4 us (3%)
  between operations  15.9 us (3%)
    unnamed x7, waiting for transfers between devices  228 us
    psum x1, waiting for transfers between devices, reduce_grads(): lax.psum(row_parts[0].astype(jnp.bfloat16), 'dp').astype(jnp.float32)  111 us
    dot_general x10, matrix products, product(): jnp.einsum(form_left + ',' + form_right + '->' + form_out, left_side, rig...  38.6 us
    unnamed x99, local copies, waits for them, and re-layouts  27.9 us
    dot_general x4, matrix products, weight_grad(): lax.dot_general(rows.reshape(-1, rows.shape[-1]), grads.reshape(-1, grads...  14.7 us
    all_to_all x1, waiting for transfers between devices, local(): lax.all_to_all(grad_packed_position, 'seq', split_axis=1, concat_axis=2,...  14.5 us
    dot_general x4, matrix products, project_back(): lax.dot_general(flat, weight, (((1,), (1,)), ((), ())), preferred_element...  13.8 us
    unnamed x2, other arithmetic  12.5 us
  transfers between devices with their start and end apart: 8, of which 6 were waited for; matrix products, arithmetic and copies ran while one was open for 20% of the time, Pallas kernels for 0%

commit v1 on v0

v1 whole, which is shorter than its diff:
```python
import functools

import jax
import jax.numpy as jnp
from jax import lax
from jax.experimental import pallas as pl
from jax.experimental.pallas import tpu as pltpu
from jax.sharding import PartitionSpec as P

HEADS = 8
HEAD_DIM = 72
F = 16
SIDE = 4
NZ = 8
BLOCKS = 16
WIDE = 2304
HALF = 1152
PIECE = 384
VMEM_LIMIT = 60 * 1024 * 1024


def remote(src, dst, send, recv, device):
    return pltpu.make_async_remote_copy(
        src_ref=src,
        dst_ref=dst,
        send_sem=send,
        recv_sem=recv,
        device_id=device,
        device_id_type=pl.DeviceIdType.MESH,
    )


def greet(devices):
    barrier = pltpu.get_barrier_semaphore()
    for device in devices:
        pl.semaphore_signal(barrier, inc=1, device_id=device, device_id_type=pl.DeviceIdType.MESH)
    pl.semaphore_wait(barrier, len(devices))


def exchange_kernel(in_ref, out_ref, own_sem, send_sems, recv_sems):
    dp, me = lax.axis_index("dp"), lax.axis_index("seq")
    n = SIDE * SIDE
    own = pltpu.make_async_copy(in_ref.at[me], out_ref.at[me], own_sem)
    own.start()
    greet([(dp, lax.rem(me + d, n)) for d in range(1, n)])

    def out_copy(d):
        to = lax.rem(me + d, n)
        return remote(in_ref.at[to], out_ref.at[me], send_sems.at[d], recv_sems.at[d], (dp, to))

    for d in range(1, n):
        out_copy(d).start()
    for d in range(1, n):
        source = lax.rem(me + n - d, n)
        remote(
            in_ref.at[source], out_ref.at[source], send_sems.at[d], recv_sems.at[d], (dp, source)
        ).wait_recv()
    for d in range(1, n):
        out_copy(d).wait_send()
    own.wait()


def exchange(blocks, collective_id):
    n = SIDE * SIDE
    return pl.pallas_call(
        exchange_kernel,
        out_shape=jax.ShapeDtypeStruct(blocks.shape, blocks.dtype),
        in_specs=[pl.BlockSpec(memory_space=pltpu.VMEM)],
        out_specs=pl.BlockSpec(memory_space=pltpu.VMEM),
        scratch_shapes=[
            pltpu.SemaphoreType.DMA,
            pltpu.SemaphoreType.DMA((n,)),
            pltpu.SemaphoreType.DMA((n,)),
        ],
        compiler_params=pltpu.CompilerParams(
            collective_id=collective_id, has_side_effects=True, vmem_limit_bytes=VMEM_LIMIT
        ),
    )(blocks)


def plus(*refs):
    total = refs[0].astype(jnp.float32)
    for ref in refs[1:]:
        total = total + ref.astype(jnp.float32)
    return total.astype(jnp.bfloat16)


CUTS = ((0, 640), (640, 512))
LAST_CUTS = (((0, 384), (384, 256)), ((0, 256), (256, 256)))
DMA_COUNTS = (
    (BLOCKS, 2),
    (2, 2, 2),
    (2, 2, SIDE),
    (2, 2),
    (2, 2),
)


class Place:
    def __init__(self):
        dp, seq = lax.axis_index("dp"), lax.axis_index("seq")
        self.dp, self.seq = dp, seq
        self.z, self.c = lax.div(dp, 2), lax.rem(dp, 2)
        self.y, self.x = lax.div(seq, SIDE), lax.rem(seq, SIDE)
        self.twin = (self.z * 2 + 1 - self.c, seq)

    def neighbour(self, axis, dirn):
        step = 1 if dirn == 0 else SIDE - 1
        if axis == 0:
            return (self.dp, self.y * SIDE + lax.rem(self.x + step, SIDE))
        return (self.dp, lax.rem(self.y + step, SIDE) * SIDE + self.x)

    def along_z(self, d):
        return (lax.rem(self.z + d, NZ) * 2 + self.c, self.seq)

    def friends(self):
        return (
            [self.twin]
            + [self.neighbour(axis, dirn) for axis in range(2) for dirn in range(2)]
            + [self.along_z(d) for d in range(1, NZ)]
        )


class Reduction:
    def __init__(self, place, grads, buffers, sems):
        self.place, self.grads = place, grads
        self.acc, self.core_in, self.near, self.far, self.near_last, self.far_last = buffers
        (
            self.core_send,
            self.core_recv,
            self.near_send,
            self.near_recv,
            self.far_send,
            self.far_recv,
            self.near_last_send,
            self.near_last_recv,
            self.far_last_send,
            self.far_last_recv,
        ) = sems

    def lanes(self, part):
        return pl.ds(CUTS[part][0], CUTS[part][1])

    def lanes_of(self, part, core):
        return pl.ds(pl.multiple_of(core * HALF + CUTS[part][0], 128), CUTS[part][1])

    def block(self, part, j, d):
        at = self.place
        if part == 0:
            return j * SIDE + lax.rem(at.x + d, SIDE)
        return lax.rem(at.y + d, SIDE) * SIDE + j

    def core_copy(self, part, b):
        at = self.place
        return remote(
            self.grads.at[b, :, self.lanes_of(part, 1 - at.c)],
            self.core_in.at[b, :, self.lanes(part)],
            self.core_send.at[b, part],
            self.core_recv.at[b, part],
            at.twin,
        )

    def near_copy(self, part, dirn, k, b):
        return remote(
            self.acc.at[b, :, self.lanes(part)],
            self.near.at[part, dirn, k, :, pl.ds(0, CUTS[part][1])],
            self.near_send.at[part, dirn, k],
            self.near_recv.at[part, dirn, k],
            self.place.neighbour(part, dirn),
        )

    def far_copy(self, part, dirn, j, b):
        return remote(
            self.acc.at[b, :, self.lanes(part)],
            self.far.at[part, dirn, j, :, pl.ds(0, CUTS[part][1])],
            self.far_send.at[part, dirn, j],
            self.far_recv.at[part, dirn, j],
            self.place.neighbour(part, dirn),
        )

    def last_lanes(self, part, dirn):
        start, width = LAST_CUTS[part][dirn]
        return pl.ds(CUTS[part][0] + start, width)

    def near_last_copy(self, part, dirn, b):
        width = LAST_CUTS[part][dirn][1]
        return remote(
            self.acc.at[b, :, self.last_lanes(part, dirn)],
            self.near_last.at[part, dirn, :, pl.ds(0, width)],
            self.near_last_send.at[part, dirn],
            self.near_last_recv.at[part, dirn],
            self.place.neighbour(1 - part, dirn),
        )

    def far_last_copy(self, part, dirn, b):
        return remote(
            self.acc.at[b, :, self.lanes(part)],
            self.far_last.at[part, dirn, :, pl.ds(0, CUTS[part][1])],
            self.far_last_send.at[part, dirn],
            self.far_last_recv.at[part, dirn],
            self.place.neighbour(1 - part, dirn),
        )

    def gather(self, part, b, *more):
        self.core_copy(part, b).wait_recv()
        lanes = self.lanes(part)
        mine = self.grads[b, :, self.lanes_of(part, self.place.c)]
        self.acc[b, :, lanes] = plus(mine, self.core_in[b, :, lanes], *more)

    def start(self):
        for d in (2, 1, 3, 0):

            @pl.loop(0, SIDE)
            def _(j):
                for part in range(2):
                    self.core_copy(part, self.block(part, j, d)).start()

    def first(self):
        for dirn in range(2):

            @pl.loop(0, 2)
            def _(k):
                for part in range(2):
                    b = self.block(part, 2 * dirn + k, 2)
                    self.gather(part, b)
                    self.near_copy(part, dirn, k, b).start()

    def second(self):
        for dirn in range(2):

            @pl.loop(0, 2)
            def _(k):
                for part in range(2):
                    j = 2 * (1 - dirn) + k
                    b = self.block(part, j, 1 + 2 * dirn)
                    self.gather(part, b)
                    self.far_copy(part, dirn, j, b).start()

    def third(self):
        for dirn in range(2):

            @pl.loop(0, 2)
            def _(k):
                for part in range(2):
                    j = 2 * dirn + k
                    b = self.block(part, j, 1 + 2 * dirn)
                    self.near_copy(part, dirn, k, b).wait_recv()
                    self.gather(part, b, self.near[part, dirn, k, :, pl.ds(0, CUTS[part][1])])
                    self.far_copy(part, dirn, j, b).start()

    def finish(self, part, d):
        at = self.place
        b = self.block(1 - part, (at.x, at.y)[part], d)
        j = lax.rem((at.y, at.x)[part] + d, SIDE)
        for dirn in range(2):
            self.far_copy(part, dirn, j, b).wait_recv()
        width = pl.ds(0, CUTS[part][1])
        self.gather(part, b, self.far[part, 0, j, :, width], self.far[part, 1, j, :, width])
        return b

    def fourth(self):
        for part in range(2):
            b = self.finish(part, 2)
            for dirn in range(2):
                self.near_last_copy(part, dirn, b).start()

    def fifth(self):
        for dirn in range(2):
            for part in range(2):
                b = self.finish(part, 1 + 2 * dirn)
                self.near_last_copy(part, dirn, b).wait_recv()
                lanes = self.last_lanes(part, dirn)
                width = LAST_CUTS[part][dirn][1]
                self.acc[b, :, lanes] = plus(
                    self.acc[b, :, lanes], self.near_last[part, dirn, :, pl.ds(0, width)]
                )
                self.far_last_copy(part, dirn, b).start()

    def sixth(self, final, offset):
        for part in range(2):
            b = self.finish(part, 0)
            for dirn in range(2):
                self.far_last_copy(part, dirn, b).wait_recv()
            start, width = CUTS[part]
            final[:, offset + start : offset + start + width] = plus(
                self.acc[b, :, self.lanes(part)],
                self.far_last[part, 0, :, pl.ds(0, width)],
                self.far_last[part, 1, :, pl.ds(0, width)],
            )

    def settle(self):
        for part in range(2):

            @pl.loop(0, BLOCKS)
            def _(b):
                self.core_copy(part, b).wait_send()

            for dirn in range(2):

                @pl.loop(0, 2)
                def _(k):
                    self.near_copy(part, dirn, k, 0).wait_send()

                @pl.loop(0, SIDE)
                def _(j):
                    self.far_copy(part, dirn, j, 0).wait_send()

                self.near_last_copy(part, dirn, 0).wait_send()
                self.far_last_copy(part, dirn, 0).wait_send()


def reduction_buffers():
    half = jnp.bfloat16
    return [
        pltpu.VMEM((BLOCKS, 72, HALF), half),
        pltpu.VMEM((BLOCKS, 72, HALF), half),
        pltpu.VMEM((2, 2, 2, 72, 640), half),
        pltpu.VMEM((2, 2, SIDE, 72, 640), half),
        pltpu.VMEM((2, 2, 72, 640), half),
        pltpu.VMEM((2, 2, 72, 640), half),
    ]


def reduction_sems():
    return [pltpu.SemaphoreType.DMA(counts) for counts in DMA_COUNTS for _ in range(2)]


def over_z(at, final, out, z_in, z_sum, z_out, z_pair, sems):
    z_send, z_recv, zo_send, zo_recv, zp_send, zp_recv = sems
    z, c = at.z, at.c

    def piece(p):
        return pl.ds(pl.multiple_of(256 * p + 128 * lax.div(p, NZ - 1), 128), PIECE)

    def z_copy(d):
        return remote(
            final.at[:, piece(lax.rem(z + d, NZ))],
            z_in.at[d],
            z_send.at[d],
            z_recv.at[d],
            at.along_z(d),
        )

    def zo_copy(d):
        return remote(z_sum, z_out.at[d], zo_send.at[d], zo_recv.at[d], at.along_z(d))

    def zp_copy(d):
        source = z_sum if d == 0 else z_out.at[d]
        return remote(source, z_pair.at[d], zp_send.at[d], zp_recv.at[d], at.twin)

    for d in range(1, NZ):
        z_copy(d).start()
    total = final[:, piece(z)].astype(jnp.float32)
    for d in range(1, NZ):
        z_copy(d).wait_recv()
        total = total + z_in[d].astype(jnp.float32)
    z_sum[...] = total.astype(jnp.bfloat16)
    for d in range(1, NZ):
        zo_copy(d).start()
    zp_copy(0).start()
    out[c, :, piece(z)] = z_sum[...]
    for d in range(1, NZ):
        zo_copy(d).wait_recv()
        zp_copy(d).start()
        out[c, :, piece(lax.rem(z + NZ - d, NZ))] = z_out[d]
    for d in range(NZ):
        zp_copy(d).wait_recv()
        out[1 - c, :, piece(lax.rem(z + NZ - d, NZ))] = z_pair[d]
    for d in range(NZ):
        if d:
            z_copy(d).wait_send()
            zo_copy(d).wait_send()
        zp_copy(d).wait_send()


def z_scratch():
    half = jnp.bfloat16
    return [
        pltpu.VMEM((72, WIDE), half),
        pltpu.VMEM((NZ, 72, PIECE), half),
        pltpu.VMEM((72, PIECE), half),
        pltpu.VMEM((NZ, 72, PIECE), half),
        pltpu.VMEM((NZ, 72, PIECE), half),
    ]


def z_sems():
    return [pltpu.SemaphoreType.DMA((NZ,))] * 6


def reduce_kernel(temporal, spatial, out, *scratch):
    at = Place()
    greet(at.friends())
    final, z_buffers, scratch = scratch[0], scratch[1:5], scratch[5:]
    z_sem, scratch = scratch[:6], scratch[6:]
    parts = []
    for grads in (temporal, spatial):
        parts.append(Reduction(at, grads, scratch[:6], scratch[6:16]))
        scratch = scratch[16:]
    one, two = parts
    one.start()
    two.start()
    one.first()
    one.second()
    two.first()
    one.third()
    two.second()
    one.fourth()
    two.third()
    one.fifth()
    two.fourth()
    one.sixth(final, 0)
    two.fifth()
    two.sixth(final, HALF)
    over_z(at, final, out, *z_buffers, z_sem)
    one.settle()
    two.settle()


def reduce_weights(temporal, spatial, collective_id):
    return pl.pallas_call(
        reduce_kernel,
        out_shape=jax.ShapeDtypeStruct((2, 72, WIDE), jnp.bfloat16),
        in_specs=[pl.BlockSpec(memory_space=pltpu.VMEM)] * 2,
        out_specs=pl.BlockSpec(memory_space=pltpu.VMEM),
        scratch_shapes=z_scratch()
        + z_sems()
        + reduction_buffers()
        + reduction_sems()
        + reduction_buffers()
        + reduction_sems(),
        compiler_params=pltpu.CompilerParams(
            collective_id=collective_id, has_side_effects=True, vmem_limit_bytes=VMEM_LIMIT
        ),
    )(temporal, spatial)


NORM_EPS = 1e-06
MASKED = -1e30
ROWS = 320
SPAN = 20
D = 1152
INNER = 576
QKV = 1728
STEP = 32
UNROLL = 2
SHARP = HEAD_DIM ** (-0.5)
NN = (((1,), (0,)), ((), ()))
NT = (((1,), (1,)), ((), ()))
TN = (((0,), (0,)), ((), ()))


def matmul(left, right, dims=NN):
    return lax.dot_general(left, right, dims, preferred_element_type=jnp.float32)


def columns(total, width=256):
    return [(start, min(width, total - start)) for start in range(0, total, width)]


def by_rows(body):
    @pl.loop(0, ROWS, step=STEP)
    def _(start):
        body(pl.ds(pl.multiple_of(start, STEP), STEP))


def normalise(source):
    average = jnp.mean(source, axis=-1, keepdims=True)
    centred = source - average
    variance = jnp.mean(centred * centred, axis=-1, keepdims=True)
    spread = lax.rsqrt(variance + NORM_EPS)
    return centred * spread, spread


def modulate(source_ref, mod_ref, first, out_ref):
    shift = mod_ref[first : first + 1, :]
    gain = 1.0 + mod_ref[first + 1 : first + 2, :]

    def body(rows):
        unit, _ = normalise(source_ref[rows, :].astype(jnp.float32))
        out_ref[rows, :] = (unit * gain + shift).astype(jnp.bfloat16)

    by_rows(body)


def norm_pullback(source, upstream, gain):
    unit, spread = normalise(source)
    grad = upstream * gain
    along = jnp.mean(grad * unit, axis=-1, keepdims=True)
    return spread * (grad - jnp.mean(grad, axis=-1, keepdims=True) - unit * along)


def project_rows(rows_ref, weight_ref, out_ref):
    for start, width in columns(weight_ref.shape[0]):
        cols = slice(start, start + width)
        out_ref[:, cols] = matmul(rows_ref[...], weight_ref[cols, :], NT).astype(out_ref.dtype)


def spread_heads(wide_ref, heads_ref, count):
    for i in range(count):
        heads_ref[i] = wide_ref[:, i * HEAD_DIM : (i + 1) * HEAD_DIM]


def join_heads(heads_ref, wide_ref, count):
    for i in range(count):
        wide_ref[:, i * HEAD_DIM : (i + 1) * HEAD_DIM] = heads_ref[i]


def from_blocks(blocks_ref, flat_ref):
    for i in range(BLOCKS):
        flat_ref[i * SPAN : (i + 1) * SPAN, :] = blocks_ref[i].astype(jnp.float32)


def to_block(flat_ref, i):
    return flat_ref[i * SPAN : (i + 1) * SPAN, :].astype(jnp.bfloat16)


def attend_spatial(heads, mixed_heads):
    def body(h, _):
        scores = matmul(heads[h], heads[HEADS + h], NT) * SHARP
        exponent = jnp.exp(scores - jnp.max(scores, axis=-1, keepdims=True))
        soft = exponent / jnp.sum(exponent, axis=-1, keepdims=True)
        mixed_heads[h] = matmul(soft.astype(jnp.bfloat16), heads[2 * HEADS + h]).astype(jnp.bfloat16)
        return 0

    lax.fori_loop(0, HEADS, body, 0, unroll=UNROLL)


def attend_back(heads, grad_heads, out_heads, keep=None, attended=None):
    def body(h, _):
        queries, keys, values = heads[h], heads[HEADS + h], heads[2 * HEADS + h]
        scores = matmul(keys, queries, NT) * SHARP
        if keep is not None:
            scores = jnp.where(keep[...] > 0.0, scores, MASKED)
        exponent = jnp.exp(scores - jnp.max(scores, axis=0, keepdims=True))
        soft = exponent / jnp.sum(exponent, axis=0, keepdims=True)
        soft_rounded = soft.astype(jnp.bfloat16)
        if attended is not None:
            rows = pl.ds(pl.multiple_of(h * HEAD_DIM, 8), HEAD_DIM)
            attended[rows, :] = matmul(values, soft_rounded, TN)
        upstream = grad_heads[h]
        raw = matmul(values, upstream, NT)
        centred = raw - jnp.sum(raw * soft, axis=0, keepdims=True)
        grad_scores = (soft * centred * SHARP).astype(jnp.bfloat16)
        out_heads[2 * HEADS + h] = matmul(soft_rounded, upstream).astype(jnp.bfloat16)
        out_heads[HEADS + h] = matmul(grad_scores, queries).astype(jnp.bfloat16)
        out_heads[h] = matmul(grad_scores, keys, TN).astype(jnp.bfloat16)
        return 0

    lax.fori_loop(0, HEADS, body, 0, unroll=UNROLL)


def weight_blocks(tall, packed_grads, inner_tall, cot, low, high, grads):
    for start, width in columns(QKV):
        cols = slice(start, start + width)
        product = matmul(tall[...], packed_grads[:, cols])
        grads[:, :, cols] = product.reshape(BLOCKS, 72, width).astype(jnp.bfloat16)
    low[...] = jnp.zeros_like(low)
    high[...] = jnp.zeros_like(high)
    for s in range(BLOCKS):
        rows = inner_tall[s * 36 : (s + 1) * 36, :]
        low[s * 72 : s * 72 + 36, :] = rows
        high[s * 72 + 36 : (s + 1) * 72, :] = rows
    low_rows, high_rows = low[...].astype(jnp.bfloat16), high[...].astype(jnp.bfloat16)
    for start, width in ((0, 192), (192, 192), (384, 192)):
        product = matmul(low_rows, cot[:, start : start + width]) + matmul(
            high_rows, cot[:, INNER + start : INNER + start + width]
        )
        grads[:, :, QKV + start : QKV + start + width] = product.reshape(BLOCKS, 72, width).astype(
            jnp.bfloat16
        )


def transposed(rows_ref, tall_ref):
    for start, width in columns(rows_ref.shape[1], 128):
        cols = slice(start, start + width)
        tall_ref[cols, :] = rows_ref[:, cols].T


def front_kernel(tokens, mod, w_qkv, w_out, packed, mixed, blocks, normed, heads, mixed_heads, flat):
    modulate(tokens, mod, 0, normed)
    project_rows(normed, w_qkv, packed)
    spread_heads(packed, heads, 3 * HEADS)
    attend_spatial(heads, mixed_heads)
    join_heads(mixed_heads, mixed, HEADS)
    gate = mod[2:3, :]
    for start, width in columns(D):
        cols = slice(start, start + width)
        product = matmul(mixed[...], w_out[:, cols])
        flat[:, cols] = tokens[:, cols].astype(jnp.float32) + gate[:, cols] * product
    for i in range(BLOCKS):
        blocks[i] = to_block(flat, i)


def middle_kernel(
    resid_blocks,
    cot_blocks,
    lengths,
    mod,
    w_qkv,
    w_out,
    grad_blocks,
    grads,
    flat,
    cot_flat,
    normed,
    packed,
    heads,
    scaled,
    grad_attended,
    grad_heads,
    out_heads,
    keep,
    attended,
    packed_grads,
    tall,
    low,
    high,
    upstream,
):
    limit = lengths[0].astype(jnp.float32)

    def frame_of(index):
        return jnp.floor((index + 0.5) * (1.0 / SPAN))

    keys = lax.broadcasted_iota(jnp.int32, (ROWS, 1), 0).astype(jnp.float32)
    queries = lax.broadcasted_iota(jnp.int32, (1, ROWS), 1).astype(jnp.float32)
    key_frame, query_frame = frame_of(keys), frame_of(queries)
    same = (keys - SPAN * key_frame) == (queries - SPAN * query_frame)
    keep[...] = jnp.where(same & (key_frame < limit), 1.0, 0.0)

    from_blocks(cot_blocks, cot_flat)
    gate = mod[5:6, :]

    def scale_cot(rows):
        start = rows.start
        index = lax.broadcasted_iota(jnp.int32, (STEP, 1), 0) + start
        live = jnp.where(frame_of(index.astype(jnp.float32)) < limit, 1.0, 0.0)
        masked = cot_flat[rows, :] * live
        cot_flat[rows, :] = masked
        scaled[rows, :] = (gate * masked).astype(jnp.bfloat16)

    by_rows(scale_cot)
    grad_attended[...] = matmul(scaled[...], w_out[...], NT).astype(jnp.bfloat16)
    spread_heads(grad_attended, grad_heads, HEADS)

    from_blocks(resid_blocks, flat)
    modulate(flat, mod, 3, normed)
    project_rows(normed, w_qkv, packed)
    spread_heads(packed, heads, 3 * HEADS)
    attend_back(heads, grad_heads, out_heads, keep, attended)
    join_heads(out_heads, packed_grads, 3 * HEADS)
    pull_back(packed_grads, w_qkv, flat, mod, 3, cot_flat, upstream)
    for i in range(BLOCKS):
        grad_blocks[i] = to_block(cot_flat, i)
    transposed(normed, tall)
    weight_blocks(tall, packed_grads, attended, scaled, low, high, grads)


def pull_back(packed_grads, w_qkv, source, mod, first, into, upstream):
    gain = 1.0 + mod[first + 1 : first + 2, :]
    for start, width in columns(D):
        cols = slice(start, start + width)
        upstream[:, cols] = matmul(packed_grads[...], w_qkv[:, cols])

    def body(rows):
        into[rows, :] = into[rows, :] + norm_pullback(
            source[rows, :].astype(jnp.float32), upstream[rows, :], gain
        )

    by_rows(body)


def back_kernel(
    tokens,
    grad_blocks,
    packed,
    mixed,
    mod,
    w_qkv,
    w_out,
    grad_tokens,
    grads,
    flat,
    normed,
    heads,
    scaled,
    grad_mixed,
    grad_heads,
    out_heads,
    mixed_tall,
    packed_grads,
    tall,
    low,
    high,
    upstream,
):
    from_blocks(grad_blocks, flat)
    gate = mod[2:3, :]

    def scale(rows):
        scaled[rows, :] = (gate * flat[rows, :]).astype(jnp.bfloat16)

    by_rows(scale)
    grad_mixed[...] = matmul(scaled[...], w_out[...], NT).astype(jnp.bfloat16)
    spread_heads(grad_mixed, grad_heads, HEADS)
    spread_heads(packed, heads, 3 * HEADS)
    attend_back(heads, grad_heads, out_heads)
    join_heads(out_heads, packed_grads, 3 * HEADS)
    modulate(tokens, mod, 0, normed)
    transposed(normed, tall)
    mixed_tall[...] = mixed[...].astype(jnp.float32).T
    weight_blocks(tall, packed_grads, mixed_tall, scaled, low, high, grads)
    pull_back(packed_grads, w_qkv, tokens, mod, 0, flat, upstream)

    def last(rows):
        grad_tokens[rows, :] = flat[rows, :].astype(jnp.bfloat16)

    by_rows(last)


HALF16 = jnp.bfloat16


def vmem(shape, dtype=HALF16):
    return pltpu.VMEM(shape, dtype)


def whole(count):
    return [pl.BlockSpec(memory_space=pltpu.VMEM)] * count


def front(tokens, mod, w_qkv, w_out):
    return pl.pallas_call(
        front_kernel,
        out_shape=(
            jax.ShapeDtypeStruct((ROWS, QKV), HALF16),
            jax.ShapeDtypeStruct((ROWS, INNER), HALF16),
            jax.ShapeDtypeStruct((BLOCKS, SPAN, D), HALF16),
        ),
        in_specs=whole(4),
        out_specs=tuple(whole(3)),
        scratch_shapes=[
            vmem((ROWS, D)),
            vmem((3 * HEADS, ROWS, HEAD_DIM)),
            vmem((HEADS, ROWS, HEAD_DIM)),
            vmem((ROWS, D), jnp.float32),
        ],
        compiler_params=pltpu.CompilerParams(vmem_limit_bytes=VMEM_LIMIT),
    )(tokens, mod, w_qkv, w_out)


def middle(resid_blocks, cot_blocks, lengths, mod, w_qkv, w_out):
    wide = jnp.float32
    return pl.pallas_call(
        middle_kernel,
        out_shape=(
            jax.ShapeDtypeStruct((BLOCKS, SPAN, D), HALF16),
            jax.ShapeDtypeStruct((BLOCKS, 72, WIDE), HALF16),
        ),
        in_specs=whole(2) + [pl.BlockSpec(memory_space=pltpu.SMEM)] + whole(3),
        out_specs=tuple(whole(2)),
        scratch_shapes=[
            vmem((ROWS, D), wide),
            vmem((ROWS, D), wide),
            vmem((ROWS, D)),
            vmem((ROWS, QKV)),
            vmem((3 * HEADS, ROWS, HEAD_DIM)),
            vmem((ROWS, D)),
            vmem((ROWS, INNER)),
            vmem((HEADS, ROWS, HEAD_DIM)),
            vmem((3 * HEADS, ROWS, HEAD_DIM)),
            vmem((ROWS, ROWS), wide),
            vmem((INNER, ROWS), wide),
            vmem((ROWS, QKV)),
            vmem((D, ROWS)),
            vmem((D, ROWS), wide),
            vmem((D, ROWS), wide),
            vmem((ROWS, D), wide),
        ],
        compiler_params=pltpu.CompilerParams(vmem_limit_bytes=VMEM_LIMIT),
    )(resid_blocks, cot_blocks, lengths, mod, w_qkv, w_out)


def back(tokens, grad_blocks, packed, mixed, mod, w_qkv, w_out):
    wide = jnp.float32
    return pl.pallas_call(
        back_kernel,
        out_shape=(
            jax.ShapeDtypeStruct((ROWS, D), HALF16),
            jax.ShapeDtypeStruct((BLOCKS, 72, WIDE), HALF16),
        ),
        in_specs=whole(7),
        out_specs=tuple(whole(2)),
        scratch_shapes=[
            vmem((ROWS, D), wide),
            vmem((ROWS, D)),
            vmem((3 * HEADS, ROWS, HEAD_DIM)),
            vmem((ROWS, D)),
            vmem((ROWS, INNER)),
            vmem((HEADS, ROWS, HEAD_DIM)),
            vmem((3 * HEADS, ROWS, HEAD_DIM)),
            vmem((INNER, ROWS), wide),
            vmem((ROWS, QKV)),
            vmem((D, ROWS)),
            vmem((D, ROWS), wide),
            vmem((D, ROWS), wide),
            vmem((ROWS, D), wide),
        ],
        compiler_params=pltpu.CompilerParams(vmem_limit_bytes=VMEM_LIMIT),
    )(tokens, grad_blocks, packed, mixed, mod, w_qkv, w_out)


def unpack_grads(summed, item):
    left, right = (half[:, item * HALF : (item + 1) * HALF] for half in (summed[0], summed[1]))
    tall = right[:, QKV - HALF :]
    return (
        jnp.concatenate([left, right[:, : QKV - HALF]], axis=-1),
        jnp.concatenate([tall[:36], tall[36:]], axis=-1),
    )


def local(
    tokens,
    cotangent,
    modulation,
    lengths,
    w_spatial_qkv,
    w_spatial_out,
    w_temporal_qkv,
    w_temporal_out,
):
    mod = modulation[0]
    source = tokens.reshape(ROWS, D)
    w_spatial_qkv, w_temporal_qkv = w_spatial_qkv.T, w_temporal_qkv.T
    cot_place = exchange(cotangent.reshape(BLOCKS, SPAN, D), 0)
    packed, mixed, residual = front(source, mod, w_spatial_qkv, w_spatial_out)
    residual_place = exchange(residual, 1)
    grad_residual, temporal = middle(
        residual_place, cot_place, lengths, mod, w_temporal_qkv, w_temporal_out
    )
    grad_home = exchange(grad_residual, 2)
    grad_tokens, spatial = back(source, grad_home, packed, mixed, mod, w_spatial_qkv, w_spatial_out)
    summed = reduce_weights(temporal, spatial, 3)
    temporal_qkv, temporal_out = unpack_grads(summed, 0)
    spatial_qkv, spatial_out = unpack_grads(summed, 1)
    return (
        grad_tokens.reshape(tokens.shape),
        spatial_qkv,
        spatial_out,
        temporal_qkv,
        temporal_out,
    )


def solution(mesh):
    placed = (
        P("dp", "seq", None, None),
        P("dp", "seq", None, None),
        P("dp", None, None),
        P("dp"),
        P(),
        P(),
        P(),
        P(),
    )
    return jax.shard_map(
        local,
        mesh=mesh,
        in_specs=placed,
        out_specs=(
            P("dp", "seq", None, None),
            P("seq", None),
            P("seq", None),
            P("seq", None),
            P("seq", None),
        ),
        check_vma=False,
    )
```

time: 584 us -> 206 us (0.35)
  waiting for transfers between devices: 358 us -> 0 us
  Pallas kernels: 0 us -> 198 us
  matrix products: 81.4 us -> 0 us
  local copies, waits for them, and re-layouts: 77 us -> 4.77 us
  starting transfers between devices: 26.1 us -> 0 us
  other arithmetic: 19.4 us -> 1.59 us
  between operations: 15.9 us -> 1.34 us
    unnamed x7 -> x0, waiting for transfers between devices: 228 us -> none
    pallas_call x0 -> x7, Pallas kernels: none -> 198 us  [the longest x1 75.7 us: reduce_weights(): pl.pallas_call(reduce_kernel, out_shape=jax.ShapeDtypeStruct((2, 72, WIDE...]
    psum x1 -> x0, waiting for transfers between devices: 111 us -> none  [reduce_grads(): lax.psum(row_parts[0].astype(jnp.bfloat16), 'dp').astype(jnp.float32)]
    dot_general x21 -> x0, matrix products: 73.7 us -> none  [the longest x10 38.6 us: product(): jnp.einsum(form_left + ',' + form_right + '->' + form_out, left_side, rig...]
    unnamed x99 -> x1, local copies, waits for them, and re-layouts: 27.9 us -> 1.37 us
    all_to_all x4 -> x0, starting transfers between devices: 25.7 us -> none  [the longest x1 7.8 us: local(): lax.all_to_all(grad_attended, 'seq', split_axis=2, concat_axis=1, tiled=T...]
    all_to_all x4 -> x0, waiting for transfers between devices: 20.3 us -> none  [the longest x1 14.5 us: local(): lax.all_to_all(grad_packed_position, 'seq', split_axis=1, concat_axis=2,...]
    all_to_all x3 -> x0, local copies, waits for them, and re-layouts: 14.8 us -> none  [the longest x2 10.5 us: local(): lax.all_to_all(packed_time, 'seq', split_axis=2, concat_axis=1, tiled=True)]
  transfers between devices with their start and end apart: 8 -> 0, of which waited for: 6 -> 0; matrix products, arithmetic and copies ran while one was open for 20% -> 0% of each run, Pallas kernels for 0% -> 0%
where the time goes in v1:
time: 206 us
  Pallas kernels  198 us (96%)
  local copies, waits for them, and re-layouts  4.77 us (2%)
    pallas_call x1, Pallas kernels, reduce_weights(): pl.pallas_call(reduce_kernel, out_shape=jax.ShapeDtypeStruct((2, 72, WIDE...  75.7 us
    pallas_call x3, Pallas kernels, exchange(): pl.pallas_call(exchange_kernel, out_shape=jax.ShapeDtypeStruct(blocks.sha...  55.6 us
    pallas_call x1, Pallas kernels, middle(): pl.pallas_call(middle_kernel, out_shape=(jax.ShapeDtypeStruct((BLOCKS, SP...  28.5 us
    pallas_call x1, Pallas kernels, back(): pl.pallas_call(back_kernel, out_shape=(jax.ShapeDtypeStruct((ROWS, D), HA...  25.2 us
    pallas_call x1, Pallas kernels, front(): pl.pallas_call(front_kernel, out_shape=(jax.ShapeDtypeStruct((ROWS, QKV),...  13 us

profile of v1, /device:TPU:1, one launch (start us, length us, event | category | flops | bytes accessed | tf_op | source)
XLA Modules:
  0.0 205.7 jit_solution(12627829464908078285)
XLA Ops:
  1.3 1.4 copy.15
  2.6 2.1 %reshape.20.in_ref = bf16[16,20,1152]{2,1,0:T(8,128)(2,1)} reshape(bf16[1,1,320,1152]{3,2,1,0:T(8,128)(2,1)} %param.9) | data formatting | bytes 1474560 | tf_op jit(solution)/shard_map/reshape | solution.py:836
  4.8 19.5 %shard_map.121.cot_blocks = bf16[16,20,1152]{2,1,0:T(8,128)(2,1)} custom-call(bf16[16,20,1152]{2,1,0:T(8,128)(2,1)} %reshape.20.in_ref), custom_call_target="tpu_custom_call" | custom-call | tf_op jit(solution)/shard_map/pallas_call | solution.py:65
  24.3 13.0 %shard_map.119 = (bf16[320,1728]{1,0:T(8,128)(2,1)}, bf16[320,576]{1,0:T(8,128)(2,1)}, bf16[16,20,1152]{2,1,0:T(8,128)(2,1)}) custom-call(bf16[320,1152]{1,0:T(8,128)(2,1)} %bitcast.16, f32[6,1152]{1,0:T(8,128)} %bitcast.18, bf16[1728,1152]{1,0:T(8,128)(2,1)} %bitcast.13, bf16[576,1152]{1,0:T(8,128)(2,1)} %w_out.5), custom_call_target="tpu_custom_call" | custom-call | tf_op jit(solution)/shard_map/pallas_call | solution.py:734
  37.3 18.4 %shard_map.120.resid_blocks = bf16[16,20,1152]{2,1,0:T(8,128)(2,1)} custom-call(bf16[16,20,1152]{2,1,0:T(8,128)(2,1)} %get-tuple-element.12.in_ref), custom_call_target="tpu_custom_call" | custom-call | tf_op jit(solution)/shard_map/pallas_call | solution.py:65
  55.7 28.5 %shard_map.122 = (bf16[16,20,1152]{2,1,0:T(8,128)(2,1)}, bf16[16,72,2304]{2,1,0:T(8,128)(2,1)}) custom-call(bf16[16,20,1152]{2,1,0:T(8,128)(2,1)} %shard_map.120.resid_blocks, bf16[16,20,1152]{2,1,0:T(8,128)(2,1)} %shard_map.121.cot_blocks, s32[1]{0:T(128)S(6)} %copy.16.lengths, f32[6,1152]{1,0:T(8,128)} %bitcast.19, bf16[1728,1152]{1,0:T(8,128)(2,1)} %bitcast.15, ...), custom_call_target="tpu_custom_call" | custom-call | tf_op jit(solution)/shard_map/pallas_call | solution.py:755
  84.2 17.7 %shard_map.123.grad_blocks = bf16[16,20,1152]{2,1,0:T(8,128)(2,1)} custom-call(bf16[16,20,1152]{2,1,0:T(8,128)(2,1)} %get-tuple-element.13.in_ref), custom_call_target="tpu_custom_call" | custom-call | tf_op jit(solution)/shard_map/pallas_call | solution.py:65
  101.9 25.2 %shard_map.124 = (bf16[320,1152]{1,0:T(8,128)(2,1)}, bf16[16,72,2304]{2,1,0:T(8,128)(2,1)}) custom-call(bf16[320,1152]{1,0:T(8,128)(2,1)} %bitcast.17, bf16[16,20,1152]{2,1,0:T(8,128)(2,1)} %shard_map.123.grad_blocks, bf16[320,1728]{1,0:T(8,128)(2,1)} %get-tuple-element.14.packed, bf16[320,576]{1,0:T(8,128)(2,1)} %get-tuple-element.15.mixed, ...), custom_call_target="tpu_custom_call" | custom-call | tf_op jit(solution)/shard_map/pallas_call | solution.py:787
  127.1 75.7 %shard_map.125 = bf16[2,72,2304]{2,1,0:T(8,128)(2,1)} custom-call(bf16[16,72,2304]{2,1,0:T(8,128)(2,1)} %get-tuple-element.17.temporal, bf16[16,72,2304]{2,1,0:T(8,128)(2,1)} %get-tuple-element.18.spatial), custom_call_target="tpu_custom_call" | custom-call | tf_op jit(solution)/shard_map/pallas_call | solution.py:421
  202.8 1.1 slice_bitcast_fusion.1
  204.0 0.1 fusion
  204.1 0.8 pad_maximum_fusion.2
  204.9 0.8 pad_maximum_fusion
  (2 shorter events, 0.0 us)

commit v2 on v1

--- a/solution.py
+++ b/solution.py
@@ -30,52 +30,64 @@
     )
 
 
-def greet(devices):
+def hail(devices):
     barrier = pltpu.get_barrier_semaphore()
     for device in devices:
         pl.semaphore_signal(barrier, inc=1, device_id=device, device_id_type=pl.DeviceIdType.MESH)
-    pl.semaphore_wait(barrier, len(devices))
-
-
-def exchange_kernel(in_ref, out_ref, own_sem, send_sems, recv_sems):
-    dp, me = lax.axis_index("dp"), lax.axis_index("seq")
-    n = SIDE * SIDE
-    own = pltpu.make_async_copy(in_ref.at[me], out_ref.at[me], own_sem)
-    own.start()
-    greet([(dp, lax.rem(me + d, n)) for d in range(1, n)])
-
-    def out_copy(d):
-        to = lax.rem(me + d, n)
-        return remote(in_ref.at[to], out_ref.at[me], send_sems.at[d], recv_sems.at[d], (dp, to))
-
-    for d in range(1, n):
-        out_copy(d).start()
-    for d in range(1, n):
-        source = lax.rem(me + n - d, n)
-        remote(
-            in_ref.at[source], out_ref.at[source], send_sems.at[d], recv_sems.at[d], (dp, source)
-        ).wait_recv()
-    for d in range(1, n):
-        out_copy(d).wait_send()
-    own.wait()
-
-
-def exchange(blocks, collective_id):
-    n = SIDE * SIDE
-    return pl.pallas_call(
-        exchange_kernel,
-        out_shape=jax.ShapeDtypeStruct(blocks.shape, blocks.dtype),
-        in_specs=[pl.BlockSpec(memory_space=pltpu.VMEM)],
-        out_specs=pl.BlockSpec(memory_space=pltpu.VMEM),
-        scratch_shapes=[
-            pltpu.SemaphoreType.DMA,
-            pltpu.SemaphoreType.DMA((n,)),
-            pltpu.SemaphoreType.DMA((n,)),
-        ],
-        compiler_params=pltpu.CompilerParams(
-            collective_id=collective_id, has_side_effects=True, vmem_limit_bytes=VMEM_LIMIT
-        ),
-    )(blocks)
+
+
+def meet(devices):
+    pl.semaphore_wait(pltpu.get_barrier_semaphore(), len(devices))
+
+
+class Exchange:
+    def __init__(self, place, source, into, own_sem, send_sems, recv_sems):
+        self.place, self.source, self.into = place, source, into
+        self.own_sem, self.send_sems, self.recv_sems = own_sem, send_sems, recv_sems
+
+    def to(self, d):
+        return lax.rem(self.place.seq + d, BLOCKS)
+
+    def copy(self, d):
+        at = self.place
+        return remote(
+            self.source.at[self.to(d)],
+            self.into.at[at.seq],
+            self.send_sems.at[d],
+            self.recv_sems.at[d],
+            (at.dp, self.to(d)),
+        )
+
+    def own(self):
+        me = self.place.seq
+        return pltpu.make_async_copy(self.source.at[me], self.into.at[me], self.own_sem)
+
+    def start(self):
+        self.own().start()
+        for d in range(1, BLOCKS):
+            self.copy(d).start()
+
+    def arrive(self):
+        at = self.place
+        for d in range(1, BLOCKS):
+            origin = lax.rem(at.seq + BLOCKS - d, BLOCKS)
+            remote(
+                self.source.at[origin],
+                self.into.at[origin],
+                self.send_sems.at[d],
+                self.recv_sems.at[d],
+                (at.dp, origin),
+            ).wait_recv()
+        self.own().wait()
+
+    def settle(self):
+        for d in range(1, BLOCKS):
+            self.copy(d).wait_send()
+
+
+def exchange_sems():
+    dma = pltpu.SemaphoreType.DMA
+    return [dma, dma((BLOCKS,)), dma((BLOCKS,))]
 
 
 def plus(*refs):
@@ -113,6 +125,9 @@
     def along_z(self, d):
         return (lax.rem(self.z + d, NZ) * 2 + self.c, self.seq)
 
+    def line(self):
+        return [(self.dp, lax.rem(self.seq + d, BLOCKS)) for d in range(1, BLOCKS)]
+
     def friends(self):
         return (
             [self.twin]
@@ -124,7 +139,7 @@
 class Reduction:
     def __init__(self, place, grads, buffers, sems):
         self.place, self.grads = place, grads
-        self.acc, self.core_in, self.near, self.far, self.near_last, self.far_last = buffers
+        self.acc, self.near, self.far, self.near_last, self.far_last = buffers
         (
             self.core_send,
             self.core_recv,
@@ -154,7 +169,7 @@
         at = self.place
         return remote(
             self.grads.at[b, :, self.lanes_of(part, 1 - at.c)],
-            self.core_in.at[b, :, self.lanes(part)],
+            self.acc.at[b, :, self.lanes(part)],
             self.core_send.at[b, part],
             self.core_recv.at[b, part],
             at.twin,
@@ -205,7 +220,7 @@
         self.core_copy(part, b).wait_recv()
         lanes = self.lanes(part)
         mine = self.grads[b, :, self.lanes_of(part, self.place.c)]
-        self.acc[b, :, lanes] = plus(mine, self.core_in[b, :, lanes], *more)
+        self.acc[b, :, lanes] = plus(mine, self.acc[b, :, lanes], *more)
 
     def start(self):
         for d in (2, 1, 3, 0):
@@ -312,7 +327,6 @@
 def reduction_buffers():
     half = jnp.bfloat16
     return [
-        pltpu.VMEM((BLOCKS, 72, HALF), half),
         pltpu.VMEM((BLOCKS, 72, HALF), half),
         pltpu.VMEM((2, 2, 2, 72, 640), half),
         pltpu.VMEM((2, 2, SIDE, 72, 640), half),
@@ -388,53 +402,6 @@
     return [pltpu.SemaphoreType.DMA((NZ,))] * 6
 
 
-def reduce_kernel(temporal, spatial, out, *scratch):
-    at = Place()
-    greet(at.friends())
-    final, z_buffers, scratch = scratch[0], scratch[1:5], scratch[5:]
-    z_sem, scratch = scratch[:6], scratch[6:]
-    parts = []
-    for grads in (temporal, spatial):
-        parts.append(Reduction(at, grads, scratch[:6], scratch[6:16]))
-        scratch = scratch[16:]
-    one, two = parts
-    one.start()
-    two.start()
-    one.first()
-    one.second()
-    two.first()
-    one.third()
-    two.second()
-    one.fourth()
-    two.third()
-    one.fifth()
-    two.fourth()
-    one.sixth(final, 0)
-    two.fifth()
-    two.sixth(final, HALF)
-    over_z(at, final, out, *z_buffers, z_sem)
-    one.settle()
-    two.settle()
-
-
-def reduce_weights(temporal, spatial, collective_id):
-    return pl.pallas_call(
-        reduce_kernel,
-        out_shape=jax.ShapeDtypeStruct((2, 72, WIDE), jnp.bfloat16),
-        in_specs=[pl.BlockSpec(memory_space=pltpu.VMEM)] * 2,
-        out_specs=pl.BlockSpec(memory_space=pltpu.VMEM),
-        scratch_shapes=z_scratch()
-        + z_sems()
-        + reduction_buffers()
-        + reduction_sems()
-        + reduction_buffers()
-        + reduction_sems(),
-        compiler_params=pltpu.CompilerParams(
-            collective_id=collective_id, has_side_effects=True, vmem_limit_bytes=VMEM_LIMIT
-        ),
-    )(temporal, spatial)
-
-
 NORM_EPS = 1e-06
 MASKED = -1e30
 ROWS = 320
@@ -526,7 +493,7 @@
     lax.fori_loop(0, HEADS, body, 0, unroll=UNROLL)
 
 
-def attend_back(heads, grad_heads, out_heads, keep=None, attended=None):
+def attend_back(heads, grad_heads, out_heads, span, keep=None, attended=None):
     def body(h, _):
         queries, keys, values = heads[h], heads[HEADS + h], heads[2 * HEADS + h]
         scores = matmul(keys, queries, NT) * SHARP
@@ -547,7 +514,7 @@
         out_heads[h] = matmul(grad_scores, keys, TN).astype(jnp.bfloat16)
         return 0
 
-    lax.fori_loop(0, HEADS, body, 0, unroll=UNROLL)
+    lax.fori_loop(span[0], span[1], body, 0, unroll=UNROLL)
 
 
 def weight_blocks(tall, packed_grads, inner_tall, cot, low, high, grads):
@@ -577,7 +544,33 @@
         tall_ref[cols, :] = rows_ref[:, cols].T
 
 
-def front_kernel(tokens, mod, w_qkv, w_out, packed, mixed, blocks, normed, heads, mixed_heads, flat):
+def front_kernel(
+    tokens,
+    cotangent,
+    mod,
+    w_qkv,
+    w_out,
+    packed,
+    mixed,
+    resid_place,
+    cot_place,
+    normed,
+    heads,
+    mixed_heads,
+    flat,
+    resid_blocks,
+    cot_blocks,
+    *sems,
+):
+    at = Place()
+    cot_trip = Exchange(at, cot_blocks, cot_place, *sems[:3])
+    resid_trip = Exchange(at, resid_blocks, resid_place, *sems[3:])
+    hail(at.line())
+    flat[...] = cotangent[...].astype(jnp.float32)
+    for i in range(BLOCKS):
+        cot_blocks[i] = to_block(flat, i)
+    meet(at.line())
+    cot_trip.start()
     modulate(tokens, mod, 0, normed)
     project_rows(normed, w_qkv, packed)
     spread_heads(packed, heads, 3 * HEADS)
@@ -589,7 +582,12 @@
         product = matmul(mixed[...], w_out[:, cols])
         flat[:, cols] = tokens[:, cols].astype(jnp.float32) + gate[:, cols] * product
     for i in range(BLOCKS):
-        blocks[i] = to_block(flat, i)
+        resid_blocks[i] = to_block(flat, i)
+    resid_trip.start()
+    for trip in (cot_trip, resid_trip):
+        trip.arrive()
+    for trip in (cot_trip, resid_trip):
+        trip.settle()
 
 
 def middle_kernel(
@@ -599,8 +597,9 @@
     mod,
     w_qkv,
     w_out,
+    grad_place,
+    grads,
     grad_blocks,
-    grads,
     flat,
     cot_flat,
     normed,
@@ -617,7 +616,11 @@
     low,
     high,
     upstream,
+    *sems,
 ):
+    at = Place()
+    grad_trip = Exchange(at, grad_blocks, grad_place, *sems)
+    hail(at.line())
     limit = lengths[0].astype(jnp.float32)
 
     def frame_of(index):
@@ -648,13 +651,17 @@
     modulate(flat, mod, 3, normed)
     project_rows(normed, w_qkv, packed)
     spread_heads(packed, heads, 3 * HEADS)
-    attend_back(heads, grad_heads, out_heads, keep, attended)
+    attend_back(heads, grad_heads, out_heads, (0, HEADS), keep, attended)
     join_heads(out_heads, packed_grads, 3 * HEADS)
     pull_back(packed_grads, w_qkv, flat, mod, 3, cot_flat, upstream)
     for i in range(BLOCKS):
         grad_blocks[i] = to_block(cot_flat, i)
+    meet(at.line())
+    grad_trip.start()
     transposed(normed, tall)
     weight_blocks(tall, packed_grads, attended, scaled, low, high, grads)
+    grad_trip.arrive()
+    grad_trip.settle()
 
 
 def pull_back(packed_grads, w_qkv, source, mod, first, into, upstream):
@@ -679,7 +686,9 @@
     mod,
     w_qkv,
     w_out,
+    temporal,
     grad_tokens,
+    out,
     grads,
     flat,
     normed,
@@ -694,7 +703,14 @@
     low,
     high,
     upstream,
+    *scratch,
 ):
+    at = Place()
+    final, z_buffers, scratch = scratch[0], scratch[1:5], scratch[5:]
+    z_sem, scratch = scratch[:6], scratch[6:]
+    one = Reduction(at, temporal, scratch[:5], scratch[5:15])
+    two = Reduction(at, grads, scratch[15:20], scratch[20:])
+    hail(at.friends())
     from_blocks(grad_blocks, flat)
     gate = mod[2:3, :]
 
@@ -702,21 +718,40 @@
         scaled[rows, :] = (gate * flat[rows, :]).astype(jnp.bfloat16)
 
     by_rows(scale)
+    meet(at.friends())
+    one.start()
     grad_mixed[...] = matmul(scaled[...], w_out[...], NT).astype(jnp.bfloat16)
     spread_heads(grad_mixed, grad_heads, HEADS)
     spread_heads(packed, heads, 3 * HEADS)
-    attend_back(heads, grad_heads, out_heads)
+    one.first()
+    one.second()
+    attend_back(heads, grad_heads, out_heads, (0, 4))
+    one.third()
+    attend_back(heads, grad_heads, out_heads, (4, HEADS))
+    one.fourth()
     join_heads(out_heads, packed_grads, 3 * HEADS)
     modulate(tokens, mod, 0, normed)
     transposed(normed, tall)
     mixed_tall[...] = mixed[...].astype(jnp.float32).T
+    one.fifth()
     weight_blocks(tall, packed_grads, mixed_tall, scaled, low, high, grads)
+    two.start()
+    one.sixth(final, 0)
+    two.first()
+    two.second()
     pull_back(packed_grads, w_qkv, tokens, mod, 0, flat, upstream)
 
     def last(rows):
         grad_tokens[rows, :] = flat[rows, :].astype(jnp.bfloat16)
 
     by_rows(last)
+    two.third()
+    two.fourth()
+    two.fifth()
+    two.sixth(final, HALF)
+    over_z(at, final, out, *z_buffers, z_sem)
+    one.settle()
+    two.settle()
 
 
 HALF16 = jnp.bfloat16
@@ -726,28 +761,39 @@
     return pltpu.VMEM(shape, dtype)
 
 
+def talking(collective_id):
+    return pltpu.CompilerParams(
+        collective_id=collective_id, has_side_effects=True, vmem_limit_bytes=VMEM_LIMIT
+    )
+
+
 def whole(count):
     return [pl.BlockSpec(memory_space=pltpu.VMEM)] * count
 
 
-def front(tokens, mod, w_qkv, w_out):
+def front(tokens, cotangent, mod, w_qkv, w_out):
     return pl.pallas_call(
         front_kernel,
         out_shape=(
             jax.ShapeDtypeStruct((ROWS, QKV), HALF16),
             jax.ShapeDtypeStruct((ROWS, INNER), HALF16),
             jax.ShapeDtypeStruct((BLOCKS, SPAN, D), HALF16),
+            jax.ShapeDtypeStruct((BLOCKS, SPAN, D), HALF16),
         ),
-        in_specs=whole(4),
-        out_specs=tuple(whole(3)),
+        in_specs=whole(5),
+        out_specs=tuple(whole(4)),
         scratch_shapes=[
             vmem((ROWS, D)),
             vmem((3 * HEADS, ROWS, HEAD_DIM)),
             vmem((HEADS, ROWS, HEAD_DIM)),
             vmem((ROWS, D), jnp.float32),
-        ],
-        compiler_params=pltpu.CompilerParams(vmem_limit_bytes=VMEM_LIMIT),
-    )(tokens, mod, w_qkv, w_out)
+            vmem((BLOCKS, SPAN, D)),
+            vmem((BLOCKS, SPAN, D)),
+        ]
+        + exchange_sems()
+        + exchange_sems(),
+        compiler_params=talking(0),
+    )(tokens, cotangent, mod, w_qkv, w_out)
 
 
 def middle(resid_blocks, cot_blocks, lengths, mod, w_qkv, w_out):
@@ -761,6 +807,7 @@
         in_specs=whole(2) + [pl.BlockSpec(memory_space=pltpu.SMEM)] + whole(3),
         out_specs=tuple(whole(2)),
         scratch_shapes=[
+            vmem((BLOCKS, SPAN, D)),
             vmem((ROWS, D), wide),
             vmem((ROWS, D), wide),
             vmem((ROWS, D)),
@@ -777,22 +824,24 @@
             vmem((D, ROWS), wide),
             vmem((D, ROWS), wide),
             vmem((ROWS, D), wide),
-        ],
-        compiler_params=pltpu.CompilerParams(vmem_limit_bytes=VMEM_LIMIT),
+        ]
+        + exchange_sems(),
+        compiler_params=talking(1),
     )(resid_blocks, cot_blocks, lengths, mod, w_qkv, w_out)
 
 
-def back(tokens, grad_blocks, packed, mixed, mod, w_qkv, w_out):
+def back(tokens, grad_blocks, packed, mixed, mod, w_qkv, w_out, temporal):
     wide = jnp.float32
     return pl.pallas_call(
         back_kernel,
         out_shape=(
             jax.ShapeDtypeStruct((ROWS, D), HALF16),
-            jax.ShapeDtypeStruct((BLOCKS, 72, WIDE), HALF16),
+            jax.ShapeDtypeStruct((2, 72, WIDE), HALF16),
         ),
-        in_specs=whole(7),
+        in_specs=whole(8),
         out_specs=tuple(whole(2)),
         scratch_shapes=[
+            vmem((BLOCKS, 72, WIDE)),
             vmem((ROWS, D), wide),
             vmem((ROWS, D)),
             vmem((3 * HEADS, ROWS, HEAD_DIM)),
@@ -806,9 +855,15 @@
             vmem((D, ROWS), wide),
             vmem((D, ROWS), wide),
             vmem((ROWS, D), wide),
-        ],
-        compiler_params=pltpu.CompilerParams(vmem_limit_bytes=VMEM_LIMIT),
-    )(tokens, grad_blocks, packed, mixed, mod, w_qkv, w_out)
+        ]
+        + z_scratch()
+        + z_sems()
+        + reduction_buffers()
+        + reduction_sems()
+        + reduction_buffers()
+        + reduction_sems(),
+        compiler_params=talking(2),
+    )(tokens, grad_blocks, packed, mixed, mod, w_qkv, w_out, temporal)
 
 
 def unpack_grads(summed, item):
@@ -833,15 +888,15 @@
     mod = modulation[0]
     source = tokens.reshape(ROWS, D)
     w_spatial_qkv, w_temporal_qkv = w_spatial_qkv.T, w_temporal_qkv.T
-    cot_place = exchange(cotangent.reshape(BLOCKS, SPAN, D), 0)
-    packed, mixed, residual = front(source, mod, w_spatial_qkv, w_spatial_out)
-    residual_place = exchange(residual, 1)
+    packed, mixed, residual, cot_place = front(
+        source, cotangent.reshape(ROWS, D), mod, w_spatial_qkv, w_spatial_out
+    )
     grad_residual, temporal = middle(
-        residual_place, cot_place, lengths, mod, w_temporal_qkv, w_temporal_out
+        residual, cot_place, lengths, mod, w_temporal_qkv, w_temporal_out
     )
-    grad_home = exchange(grad_residual, 2)
-    grad_tokens, spatial = back(source, grad_home, packed, mixed, mod, w_spatial_qkv, w_spatial_out)
-    summed = reduce_weights(temporal, spatial, 3)
+    grad_tokens, summed = back(
+        source, grad_residual, packed, mixed, mod, w_spatial_qkv, w_spatial_out, temporal
+    )
     temporal_qkv, temporal_out = unpack_grads(summed, 0)
     spatial_qkv, spatial_out = unpack_grads(summed, 1)
     return (

time: 206 us -> 165 us (0.80)
  Pallas kernels: 198 us -> 159 us
    pallas_call x4 -> x0, Pallas kernels: 131 us -> none  [the longest x1 75.7 us: reduce_weights(): pl.pallas_call(reduce_kernel, out_shape=jax.ShapeDtypeStruct((2, 72, WIDE...]
    pallas_call x1, Pallas kernels: 25.2 us -> 88.1 us  [back(): pl.pallas_call(back_kernel, out_shape=(jax.ShapeDtypeStruct((ROWS, D), HA...]
    pallas_call x1, Pallas kernels: 13 us -> 33.6 us  [front(): pl.pallas_call(front_kernel, out_shape=(jax.ShapeDtypeStruct((ROWS, QKV),...]
    pallas_call x1, Pallas kernels: 28.5 us -> 37 us  [middle(): pl.pallas_call(middle_kernel, out_shape=(jax.ShapeDtypeStruct((BLOCKS, SP...]
    reshape x1 -> x0, local copies, waits for them, and re-layouts: 2.11 us -> none  [local(): cot_place = exchange(cotangent.reshape(BLOCKS, SPAN, D), 0)]
where the time goes in v2:
time: 165 us
  Pallas kernels  159 us (96%)
  local copies, waits for them, and re-layouts  3.6 us (2%)
    pallas_call x1, Pallas kernels, back(): pl.pallas_call(back_kernel, out_shape=(jax.ShapeDtypeStruct((ROWS, D), HA...  88.1 us
    pallas_call x1, Pallas kernels, middle(): pl.pallas_call(middle_kernel, out_shape=(jax.ShapeDtypeStruct((BLOCKS, SP...  37 us
    pallas_call x1, Pallas kernels, front(): pl.pallas_call(front_kernel, out_shape=(jax.ShapeDtypeStruct((ROWS, QKV),...  33.6 us

profile of v2, /device:TPU:1, one launch (start us, length us, event | category | flops | bytes accessed | tf_op | source)
XLA Modules:
  0.0 165.2 jit_solution(3548839510471055776)
XLA Ops:
  1.3 1.4 copy.15
  2.6 33.6 %shard_map.119 = (bf16[320,1728]{1,0:T(8,128)(2,1)}, bf16[320,576]{1,0:T(8,128)(2,1)}, bf16[16,20,1152]{2,1,0:T(8,128)(2,1)}, bf16[16,20,1152]{2,1,0:T(8,128)(2,1)}) custom-call(bf16[320,1152]{1,0:T(8,128)(2,1)} %bitcast.15, bf16[320,1152]{1,0:T(8,128)(2,1)} %bitcast.17, f32[6,1152]{1,0:T(8,128)} %bitcast.19, bf16[1728,1152]{1,0:T(8,128)(2,1)} %bitcast.12, ...), custom_call_target="tpu_custom_call" | custom-call | tf_op jit(solution)/shard_map/pallas_call | solution.py:775
  36.3 37.0 %shard_map.120 = (bf16[16,20,1152]{2,1,0:T(8,128)(2,1)}, bf16[16,72,2304]{2,1,0:T(8,128)(2,1)}) custom-call(bf16[16,20,1152]{2,1,0:T(8,128)(2,1)} %get-tuple-element.13.resid_blocks, bf16[16,20,1152]{2,1,0:T(8,128)(2,1)} %get-tuple-element.14.cot_blocks, s32[1]{0:T(128)S(6)} %copy.17.lengths, f32[6,1152]{1,0:T(8,128)} %bitcast.20, ...), custom_call_target="tpu_custom_call" | custom-call | tf_op jit(solution)/shard_map/pallas_call | solution.py:801
  73.3 88.1 %shard_map.121 = (bf16[320,1152]{1,0:T(8,128)(2,1)}, bf16[2,72,2304]{2,1,0:T(8,128)(2,1)}) custom-call(bf16[320,1152]{1,0:T(8,128)(2,1)} %bitcast.16, bf16[16,20,1152]{2,1,0:T(8,128)(2,1)} %get-tuple-element.15.grad_blocks, bf16[320,1728]{1,0:T(8,128)(2,1)} %get-tuple-element.16.packed, bf16[320,576]{1,0:T(8,128)(2,1)} %get-tuple-element.17.mixed, ...), custom_call_target="tpu_custom_call" | custom-call | tf_op jit(solution)/shard_map/pallas_call | solution.py:835
  161.4 0.0 copy-start
  161.4 1.2 slice_bitcast_fusion.1
  162.6 0.1 fusion
  162.8 0.8 pad_maximum_fusion.2
  163.5 0.8 pad_maximum_fusion
  164.4 0.0 copy-done
  164.4 0.9 copy.18
  (2 shorter events, 0.0 us)
Async XLA Ops:
  161.4 3.0 %copy-start = (bf16[320,1152]{1,0:T(8,128)(2,1)S(1)}, bf16[320,1152]{1,0:T(8,128)(2,1)}, u32[]{:S(2)}) copy-start(bf16[320,1152]{1,0:T(8,128)(2,1)} %get-tuple-element.19) | copy-start | bytes 2211844

commit v3 on v2

v3 whole, which is shorter than its diff:
```python
import jax
import jax.numpy as jnp
from jax import lax
from jax.experimental import pallas as pl
from jax.experimental.pallas import tpu as pltpu
from jax.sharding import PartitionSpec as P

HEADS = 8
HEAD_DIM = 72
F = 16
SIDE = 4
NZ = 8
BLOCKS = 16
WIDE = 2304
HALF = 1152
VMEM_LIMIT = 63 * 1024 * 1024


def remote(src, dst, send, recv, device):
    return pltpu.make_async_remote_copy(
        src_ref=src,
        dst_ref=dst,
        send_sem=send,
        recv_sem=recv,
        device_id=device,
        device_id_type=pl.DeviceIdType.MESH,
    )


def hail(devices):
    barrier = pltpu.get_barrier_semaphore()
    for device in devices:
        pl.semaphore_signal(barrier, inc=1, device_id=device, device_id_type=pl.DeviceIdType.MESH)


def meet(devices):
    pl.semaphore_wait(pltpu.get_barrier_semaphore(), len(devices))


class Exchange:
    def __init__(self, place, source, into, own_sem, send_sems, recv_sems):
        self.place, self.source, self.into = place, source, into
        self.own_sem, self.send_sems, self.recv_sems = own_sem, send_sems, recv_sems

    def to(self, d):
        return lax.rem(self.place.seq + d, BLOCKS)

    def copy(self, d):
        at = self.place
        return remote(
            self.source.at[self.to(d)],
            self.into.at[at.seq],
            self.send_sems.at[d],
            self.recv_sems.at[d],
            (at.dp, self.to(d)),
        )

    def own(self):
        me = self.place.seq
        return pltpu.make_async_copy(self.source.at[me], self.into.at[me], self.own_sem)

    def start(self):
        self.own().start()
        for d in range(1, BLOCKS):
            self.copy(d).start()

    def arrive(self):
        at = self.place
        for d in range(1, BLOCKS):
            origin = lax.rem(at.seq + BLOCKS - d, BLOCKS)
            remote(
                self.source.at[origin],
                self.into.at[origin],
                self.send_sems.at[d],
                self.recv_sems.at[d],
                (at.dp, origin),
            ).wait_recv()
        self.own().wait()

    def settle(self):
        for d in range(1, BLOCKS):
            self.copy(d).wait_send()


def exchange_sems():
    dma = pltpu.SemaphoreType.DMA
    return [dma, dma((BLOCKS,)), dma((BLOCKS,))]


def plus(*refs):
    total = refs[0].astype(jnp.float32)
    for ref in refs[1:]:
        total = total + ref.astype(jnp.float32)
    return total.astype(jnp.bfloat16)


CUTS = ((0, 640), (640, 512))
LAST_CUTS = (((0, 384), (384, 256)), ((0, 256), (256, 256)))
DMA_COUNTS = (
    (BLOCKS, 2),
    (2, 2, 2),
    (2, 2, SIDE),
    (2, 2),
    (2, 2),
)


class Place:
    def __init__(self):
        dp, seq = lax.axis_index("dp"), lax.axis_index("seq")
        self.dp, self.seq = dp, seq
        self.z, self.c = lax.div(dp, 2), lax.rem(dp, 2)
        self.y, self.x = lax.div(seq, SIDE), lax.rem(seq, SIDE)
        self.twin = (self.z * 2 + 1 - self.c, seq)

    def neighbour(self, axis, dirn):
        step = 1 if dirn == 0 else SIDE - 1
        if axis == 0:
            return (self.dp, self.y * SIDE + lax.rem(self.x + step, SIDE))
        return (self.dp, lax.rem(self.y + step, SIDE) * SIDE + self.x)

    def along_z(self, d):
        return (lax.rem(self.z + d, NZ) * 2 + self.c, self.seq)

    def line(self):
        return [(self.dp, lax.rem(self.seq + d, BLOCKS)) for d in range(1, BLOCKS)]

    def friends(self):
        return [self.twin] + self.line() + [self.along_z(d) for d in range(1, NZ)]


class Reduction:
    def __init__(self, place, grads, buffers, sems):
        self.place, self.grads = place, grads
        self.acc, self.near, self.far, self.near_last, self.far_last = buffers
        (
            self.core_send,
            self.core_recv,
            self.near_send,
            self.near_recv,
            self.far_send,
            self.far_recv,
            self.near_last_send,
            self.near_last_recv,
            self.far_last_send,
            self.far_last_recv,
        ) = sems

    def lanes(self, part):
        return pl.ds(CUTS[part][0], CUTS[part][1])

    def lanes_of(self, part, core):
        return pl.ds(pl.multiple_of(core * HALF + CUTS[part][0], 128), CUTS[part][1])

    def block(self, part, j, d):
        at = self.place
        if part == 0:
            return j * SIDE + lax.rem(at.x + d, SIDE)
        return lax.rem(at.y + d, SIDE) * SIDE + j

    def core_copy(self, part, b):
        at = self.place
        return remote(
            self.grads.at[b, :, self.lanes_of(part, 1 - at.c)],
            self.acc.at[b, :, self.lanes(part)],
            self.core_send.at[b, part],
            self.core_recv.at[b, part],
            at.twin,
        )

    def near_copy(self, part, dirn, k, b):
        return remote(
            self.acc.at[b, :, self.lanes(part)],
            self.near.at[part, dirn, k, :, pl.ds(0, CUTS[part][1])],
            self.near_send.at[part, dirn, k],
            self.near_recv.at[part, dirn, k],
            self.place.neighbour(part, dirn),
        )

    def far_copy(self, part, dirn, j, b):
        return remote(
            self.acc.at[b, :, self.lanes(part)],
            self.far.at[part, dirn, j, :, pl.ds(0, CUTS[part][1])],
            self.far_send.at[part, dirn, j],
            self.far_recv.at[part, dirn, j],
            self.place.neighbour(part, dirn),
        )

    def last_lanes(self, part, dirn):
        start, width = LAST_CUTS[part][dirn]
        return pl.ds(CUTS[part][0] + start, width)

    def near_last_copy(self, part, dirn, b):
        width = LAST_CUTS[part][dirn][1]
        return remote(
            self.acc.at[b, :, self.last_lanes(part, dirn)],
            self.near_last.at[part, dirn, :, pl.ds(0, width)],
            self.near_last_send.at[part, dirn],
            self.near_last_recv.at[part, dirn],
            self.place.neighbour(1 - part, dirn),
        )

    def far_last_copy(self, part, dirn, b):
        return remote(
            self.acc.at[b, :, self.lanes(part)],
            self.far_last.at[part, dirn, :, pl.ds(0, CUTS[part][1])],
            self.far_last_send.at[part, dirn],
            self.far_last_recv.at[part, dirn],
            self.place.neighbour(1 - part, dirn),
        )

    def gather(self, part, b, *more):
        self.core_copy(part, b).wait_recv()
        lanes = self.lanes(part)
        mine = self.grads[b, :, self.lanes_of(part, self.place.c)]
        self.acc[b, :, lanes] = plus(mine, self.acc[b, :, lanes], *more)

    def start(self):
        for d in (2, 1, 3, 0):

            @pl.loop(0, SIDE)
            def _(j):
                for part in range(2):
                    self.core_copy(part, self.block(part, j, d)).start()

    def first(self):
        for dirn in range(2):

            @pl.loop(0, 2)
            def _(k):
                for part in range(2):
                    b = self.block(part, 2 * dirn + k, 2)
                    self.gather(part, b)
                    self.near_copy(part, dirn, k, b).start()

    def second(self):
        for dirn in range(2):

            @pl.loop(0, 2)
            def _(k):
                for part in range(2):
                    j = 2 * (1 - dirn) + k
                    b = self.block(part, j, 1 + 2 * dirn)
                    self.gather(part, b)
                    self.far_copy(part, dirn, j, b).start()

    def third(self):
        for dirn in range(2):

            @pl.loop(0, 2)
            def _(k):
                for part in range(2):
                    j = 2 * dirn + k
                    b = self.block(part, j, 1 + 2 * dirn)
                    self.near_copy(part, dirn, k, b).wait_recv()
                    self.gather(part, b, self.near[part, dirn, k, :, pl.ds(0, CUTS[part][1])])
                    self.far_copy(part, dirn, j, b).start()

    def finish(self, part, d):
        at = self.place
        b = self.block(1 - part, (at.x, at.y)[part], d)
        j = lax.rem((at.y, at.x)[part] + d, SIDE)
        for dirn in range(2):
            self.far_copy(part, dirn, j, b).wait_recv()
        width = pl.ds(0, CUTS[part][1])
        self.gather(part, b, self.far[part, 0, j, :, width], self.far[part, 1, j, :, width])
        return b

    def fourth(self):
        for part in range(2):
            b = self.finish(part, 2)
            for dirn in range(2):
                self.near_last_copy(part, dirn, b).start()

    def fifth(self):
        for dirn in range(2):
            for part in range(2):
                b = self.finish(part, 1 + 2 * dirn)
                self.near_last_copy(part, dirn, b).wait_recv()
                lanes = self.last_lanes(part, dirn)
                width = LAST_CUTS[part][dirn][1]
                self.acc[b, :, lanes] = plus(
                    self.acc[b, :, lanes], self.near_last[part, dirn, :, pl.ds(0, width)]
                )
                self.far_last_copy(part, dirn, b).start()

    def sixth(self, final, offset):
        for part in range(2):
            b = self.finish(part, 0)
            for dirn in range(2):
                self.far_last_copy(part, dirn, b).wait_recv()
            start, width = CUTS[part]
            final[:, offset + start : offset + start + width] = plus(
                self.acc[b, :, self.lanes(part)],
                self.far_last[part, 0, :, pl.ds(0, width)],
                self.far_last[part, 1, :, pl.ds(0, width)],
            )

    def settle(self):
        for part in range(2):

            @pl.loop(0, BLOCKS)
            def _(b):
                self.core_copy(part, b).wait_send()

            for dirn in range(2):

                @pl.loop(0, 2)
                def _(k):
                    self.near_copy(part, dirn, k, 0).wait_send()

                @pl.loop(0, SIDE)
                def _(j):
                    self.far_copy(part, dirn, j, 0).wait_send()

                self.near_last_copy(part, dirn, 0).wait_send()
                self.far_last_copy(part, dirn, 0).wait_send()


def reduction_buffers():
    half = jnp.bfloat16
    return [
        pltpu.VMEM((BLOCKS, 72, HALF), half),
        pltpu.VMEM((2, 2, 2, 72, 640), half),
        pltpu.VMEM((2, 2, SIDE, 72, 640), half),
        pltpu.VMEM((2, 2, 72, 640), half),
        pltpu.VMEM((2, 2, 72, 640), half),
    ]


def reduction_sems():
    return [pltpu.SemaphoreType.DMA(counts) for counts in DMA_COUNTS for _ in range(2)]


class Depth:
    def __init__(self, place, final, out, offset, extra, buffers, sems):
        self.place, self.final, self.out = place, final, out
        self.offset, self.extra = offset, extra
        self.arrived, self.arrived_extra = buffers
        self.send, self.recv, self.send_extra, self.recv_extra = sems[:4]
        self.out_send, self.out_recv, self.last_send, self.last_recv = sems[4:8]
        self.pair_send, self.pair_recv = sems[8:]

    def tile(self, k):
        return pl.ds(pl.multiple_of(k * 128, 128), 128)

    def spot(self, k, core):
        return self.out.at[core, :, pl.ds(pl.multiple_of(self.offset + k * 128, 128), 128)]

    def owner(self, k):
        return (k * 2 + self.place.c, self.place.seq)

    def up(self, d):
        to = lax.rem(self.place.z + d, NZ)
        return remote(
            self.final.at[:, self.tile(to)],
            self.arrived.at[d],
            self.send.at[d],
            self.recv.at[d],
            self.owner(to),
        )

    def up_extra(self, d):
        return remote(
            self.final.at[:, self.tile(NZ)],
            self.arrived_extra.at[d],
            self.send_extra,
            self.recv_extra.at[d],
            self.owner(self.extra),
        )

    def down(self, d):
        at = self.place
        spot = self.spot(at.z, at.c)
        return remote(spot, spot, self.out_send.at[d], self.out_recv.at[d], at.along_z(d))

    def down_extra(self, d):
        at = self.place
        spot = self.spot(NZ, at.c)
        return remote(spot, spot, self.last_send.at[d], self.last_recv, self.owner((self.extra + d) % NZ))

    def across(self, d):
        at = self.place
        k = NZ if d == NZ else lax.rem(at.z + NZ - d, NZ)
        spot = self.spot(k, at.c)
        return remote(spot, spot, self.pair_send.at[d], self.pair_recv.at[d], at.twin)

    def is_extra(self):
        return self.place.z == self.extra

    def rank(self):
        return lax.rem(self.place.z + NZ - self.extra, NZ)

    def start(self):
        for d in range(1, NZ):
            self.up(d).start()

        @pl.when(jnp.logical_not(self.is_extra()))
        def _():
            self.up_extra(self.rank()).start()

    def middle(self):
        at = self.place
        total = self.final[:, self.tile(at.z)].astype(jnp.float32)
        for d in range(1, NZ):
            self.up(d).wait_recv()
            total = total + self.arrived[d].astype(jnp.float32)
        self.spot(at.z, at.c)[...] = total.astype(jnp.bfloat16)
        for d in range(1, NZ):
            self.down(d).start()

        @pl.when(self.is_extra())
        def _():
            last = self.final[:, self.tile(NZ)].astype(jnp.float32)
            for d in range(1, NZ):
                self.up_extra(d).wait_recv()
                last = last + self.arrived_extra[d].astype(jnp.float32)
            self.spot(NZ, at.c)[...] = last.astype(jnp.bfloat16)
            for d in range(1, NZ):
                self.down_extra(d).start()

        self.across(0).start()

    def end(self):
        at = self.place
        for d in range(1, NZ):
            spot = self.spot(lax.rem(at.z + NZ - d, NZ), at.c)
            remote(
                spot, spot, self.out_send.at[d], self.out_recv.at[d], at.along_z(d)
            ).wait_recv()
            self.across(d).start()

        @pl.when(jnp.logical_not(self.is_extra()))
        def _():
            self.down_extra(1).wait_recv()

        self.across(NZ).start()
        for d in range(NZ + 1):
            k = NZ if d == NZ else lax.rem(at.z + NZ - d, NZ)
            spot = self.spot(k, 1 - at.c)
            remote(
                spot, spot, self.pair_send.at[d], self.pair_recv.at[d], at.twin
            ).wait_recv()

    def settle(self):
        for d in range(1, NZ):
            self.up(d).wait_send()
            self.down(d).wait_send()
        for d in range(NZ + 1):
            self.across(d).wait_send()

        @pl.when(jnp.logical_not(self.is_extra()))
        def _():
            self.up_extra(self.rank()).wait_send()

        @pl.when(self.is_extra())
        def _():
            for d in range(1, NZ):
                self.down_extra(d).wait_send()


def depth_buffers():
    return [pltpu.VMEM((NZ, 72, 128), jnp.bfloat16)] * 2


def depth_sems():
    dma = pltpu.SemaphoreType.DMA
    return [
        dma((NZ,)),
        dma((NZ,)),
        dma,
        dma((NZ,)),
        dma((NZ,)),
        dma((NZ,)),
        dma((NZ,)),
        dma,
        dma((NZ + 1,)),
        dma((NZ + 1,)),
    ]


NORM_EPS = 1e-06
MASKED = -1e30
ROWS = 320
SPAN = 8
GROUPS = 3
GROUP = SPAN * BLOCKS
SPREAD = GROUPS * GROUP
ODD = 4
D = 1152
INNER = 576
QKV = 1728
STEP = 32
UNROLL = 2
SHARP = HEAD_DIM ** (-0.5)
SHARP2 = SHARP * 1.4426950408889634
NN = (((1,), (0,)), ((), ()))
NT = (((1,), (1,)), ((), ()))
TN = (((0,), (0,)), ((), ()))
HALF16 = jnp.bfloat16


def matmul(left, right, dims=NN):
    return lax.dot_general(left, right, dims, preferred_element_type=jnp.float32)


def columns(total, width=256):
    return [(start, min(width, total - start)) for start in range(0, total, width)]


def by_rows(body, first=0, last=ROWS, step=STEP):
    @pl.loop(first, last, step=step)
    def _(start):
        body(pl.ds(pl.multiple_of(start, step), step))


def normalise(source):
    average = jnp.mean(source, axis=-1, keepdims=True)
    centred = source - average
    variance = jnp.mean(centred * centred, axis=-1, keepdims=True)
    spread = lax.rsqrt(variance + NORM_EPS)
    return centred * spread, spread


def modulated(source, mod, first):
    unit, _ = normalise(source)
    return (unit * (1.0 + mod[first + 1]) + mod[first]).astype(HALF16)


def norm_pullback(source, upstream, gain):
    unit, spread = normalise(source)
    grad = upstream * gain
    along = jnp.mean(grad * unit, axis=-1, keepdims=True)
    return spread * (grad - jnp.mean(grad, axis=-1, keepdims=True) - unit * along)


def wide(ref_value):
    return ref_value.astype(jnp.float32)


def project_rows(rows_ref, rows, weight_ref, out_ref, out_rows):
    for start, width in columns(weight_ref.shape[0]):
        cols = slice(start, start + width)
        out_ref[out_rows, cols] = matmul(rows_ref[rows, :], weight_ref[cols, :], NT).astype(HALF16)


def spread_heads(wide_ref, heads_ref, count, rows):
    for i in range(count):
        heads_ref[i, rows] = wide_ref[rows, i * HEAD_DIM : (i + 1) * HEAD_DIM]


def softmax(scores, axis):
    exponent = jnp.exp2((scores - jnp.max(scores, axis=axis, keepdims=True)) * SHARP2)
    return exponent * (1.0 / jnp.sum(exponent, axis=axis, keepdims=True))


def attend_spatial(heads, mixed_heads, rows):
    def body(h, _):
        scores = matmul(heads[h, rows], heads[HEADS + h], NT)
        soft = softmax(scores, -1).astype(HALF16)
        mixed_heads[h, rows] = matmul(soft, heads[2 * HEADS + h]).astype(HALF16)
        return 0

    lax.fori_loop(0, HEADS, body, 0, unroll=UNROLL)


def head_back(queries, keys, values, upstream, bias=None):
    scores = matmul(keys, queries, NT)
    if bias is not None:
        scores = scores + bias
    soft = softmax(scores, 0)
    soft_rounded = soft.astype(HALF16)
    raw = matmul(values, upstream, NT)
    centred = raw - jnp.sum(raw * soft, axis=0, keepdims=True)
    grad_scores = (soft * centred).astype(HALF16)
    grad_values = matmul(soft_rounded, upstream).astype(HALF16)
    grad_keys = (matmul(grad_scores, queries) * SHARP).astype(HALF16)
    grad_queries = (matmul(grad_scores, keys, TN) * SHARP).astype(HALF16)
    return grad_queries, grad_keys, grad_values, soft_rounded


def weight_blocks(depth, tall, packed_grads, inner_tall, cot, low, high, grads):
    deep = slice(0, depth)
    for start, width in columns(QKV):
        cols = slice(start, start + width)
        product = matmul(tall[:, deep], packed_grads[deep, cols])
        grads[:, :, cols] = product.reshape(BLOCKS, 72, width).astype(HALF16)
    low[:, deep] = jnp.zeros((D, depth), jnp.float32)
    high[:, deep] = jnp.zeros((D, depth), jnp.float32)
    for s in range(BLOCKS):
        rows = inner_tall[s * 36 : (s + 1) * 36, deep]
        low[s * 72 : s * 72 + 36, deep] = rows
        high[s * 72 + 36 : (s + 1) * 72, deep] = rows
    low_rows, high_rows = low[:, deep].astype(HALF16), high[:, deep].astype(HALF16)
    for start, width in ((0, 192), (192, 192), (384, 192)):
        product = matmul(low_rows, cot[deep, start : start + width]) + matmul(
            high_rows, cot[deep, INNER + start : INNER + start + width]
        )
        grads[:, :, QKV + start : QKV + start + width] = product.reshape(BLOCKS, 72, width).astype(
            HALF16
        )


def transposed(rows_ref, count, tall_ref):
    for start, width in columns(D, 128):
        cols = slice(start, start + width)
        tall_ref[cols, 0:count] = rows_ref[0:count, cols].T


def upstream_of(packed_grads, rows, w_qkv, into, count):
    for n in range(3):
        cols = slice(n * SPREAD, (n + 1) * SPREAD)
        into[n * SPREAD : n * SPREAD + count, :] = matmul(packed_grads[rows, :], w_qkv[:, cols])


def upstream_rows(into, start, step):
    return jnp.concatenate(
        [into[pl.ds(pl.multiple_of(n * SPREAD + start, step), step), :] for n in range(3)], axis=-1
    )


def pack_odd(flat, blocks):
    flat[0:GROUP, :] = jnp.zeros((GROUP, D), jnp.float32)
    for i in range(BLOCKS):
        start = 2 * GROUP + i * ODD
        flat[i * SPAN : i * SPAN + ODD, :] = flat[start : start + ODD, :]
    blocks[2] = flat[0:GROUP, :].reshape(BLOCKS, SPAN, D).astype(HALF16)


def kernel(
    lengths,
    mod,
    tokens_far,
    cot_far,
    w_spatial_qkv_far,
    w_spatial_out_far,
    w_temporal_qkv_far,
    w_temporal_out_far,
    grad_tokens,
    out,
    tokens,
    cot,
    w_spatial_qkv,
    w_spatial_out,
    w_temporal_qkv,
    w_temporal_out,
    load_sems,
    cot_blocks,
    cot_place,
    resid_blocks,
    resid_place,
    grad_place,
    flat,
    normed,
    packed,
    heads,
    mixed_heads,
    mixed,
    normed_time,
    packed_time,
    heads_time,
    scaled,
    grad_inner,
    grad_heads,
    out_heads,
    packed_grads,
    inner_tall,
    tall,
    low,
    high,
    bias,
    grads_time,
    grads_space,
    final_time,
    final_space,
    *scratch,
):
    at = Place()
    loads = [
        pltpu.make_async_copy(far, near, load_sems.at[i])
        for i, (far, near) in enumerate(
            (
                (cot_far, cot),
                (tokens_far, tokens),
                (w_spatial_qkv_far, w_spatial_qkv),
                (w_spatial_out_far, w_spatial_out),
                (w_temporal_out_far, w_temporal_out),
                (w_temporal_qkv_far, w_temporal_qkv),
            )
        )
    ]
    for load in loads:
        load.start()
    hail(at.friends())

    taken = 0

    def take(count):
        nonlocal taken
        taken += count
        return scratch[taken - count : taken]

    def trips(source, into):
        return [Exchange(at, source.at[g], into.at[g], *take(3)) for g in range(GROUPS)]

    cot_trips = trips(cot_blocks, cot_place)
    resid_trips = trips(resid_blocks, resid_place)
    grad_trips = trips(cot_blocks, grad_place)
    one = Reduction(at, grads_time, take(5), take(10))
    two = Reduction(at, grads_space, take(5), take(10))
    one_z = Depth(at, final_time, out, 0, 0, take(2), take(10))
    two_z = Depth(at, final_space, out, HALF, 4, take(2), take(10))

    loads[0].wait()
    for g in range(2):
        rows = slice(g * GROUP, (g + 1) * GROUP)
        cot_blocks[g] = wide(cot[rows, :]).reshape(BLOCKS, SPAN, D).astype(HALF16)
    flat[2 * GROUP : ROWS, :] = wide(cot[2 * GROUP : ROWS, :])
    pack_odd(flat, cot_blocks)
    meet(at.friends())
    for trip in cot_trips:
        trip.start()

    loads[1].wait()

    def norm_rows(rows):
        normed[rows, :] = modulated(wide(tokens[rows, :]), mod, 0)

    by_rows(norm_rows)
    loads[2].wait()
    project_rows(normed, slice(0, ROWS), w_spatial_qkv, packed, slice(0, ROWS))
    spread_heads(packed, heads, 3 * HEADS, slice(0, ROWS))
    loads[3].wait()

    def residual(first, last):
        rows = slice(first, last)
        attend_spatial(heads, mixed_heads, rows)
        for h in range(HEADS):
            mixed[rows, h * HEAD_DIM : (h + 1) * HEAD_DIM] = mixed_heads[h, rows]
        for start, width in columns(D):
            cols = slice(start, start + width)
            product = matmul(mixed[rows, :], w_spatial_out[:, cols])
            flat[rows, cols] = wide(tokens[rows, cols]) + mod[2][:, cols] * product

    residual(0, GROUP)
    resid_blocks[0] = flat[0:GROUP, :].reshape(BLOCKS, SPAN, D).astype(HALF16)
    resid_trips[0].start()
    residual(GROUP, ROWS)
    resid_blocks[1] = flat[GROUP : 2 * GROUP, :].reshape(BLOCKS, SPAN, D).astype(HALF16)
    resid_trips[1].start()
    pack_odd(flat, resid_blocks)
    resid_trips[2].start()

    limit = lengths[0].astype(jnp.float32)

    def frame_of(index):
        return jnp.floor(index * (1.0 / SPAN))

    keys = lax.broadcasted_iota(jnp.int32, (GROUP, 1), 0).astype(jnp.float32)
    queries = lax.broadcasted_iota(jnp.int32, (1, GROUP), 1).astype(jnp.float32)
    same = (keys - SPAN * frame_of(keys)) == (queries - SPAN * frame_of(queries))
    bias[...] = jnp.where(same & (frame_of(keys) < limit), 0.0, MASKED)

    def masked_rows(g, start):
        index = lax.broadcasted_iota(jnp.int32, (STEP, 1), 0) + start
        live = jnp.where(frame_of(index.astype(jnp.float32)) < limit, 1.0, 0.0)
        return live * frames(cot_place, g, start)

    def frames(place, g, start):
        count = STEP // SPAN
        return wide(place[g, pl.ds(lax.div(start, SPAN), count)]).reshape(STEP, D)

    def by_group(g, body):
        @pl.loop(0, GROUP, step=STEP)
        def _(start):
            body(g, start, pl.ds(pl.multiple_of(g * GROUP + start, STEP), STEP))

    def scale_cot(g, start, rows):
        scaled[rows, :] = (mod[5] * masked_rows(g, start)).astype(HALF16)

    for g in range(GROUPS):
        cot_trips[g].arrive()
        by_group(g, scale_cot)
    loads[4].wait()
    grad_inner[...] = matmul(scaled[...], w_temporal_out[...], NT).astype(HALF16)
    spread_heads(grad_inner, grad_heads, HEADS, slice(0, SPREAD))
    for trip in cot_trips:
        trip.settle()
    loads[5].wait()

    def norm_time(g, start, rows):
        normed_time[rows, :] = modulated(frames(resid_place, g, start), mod, 3)

    def temporal(members):
        count = len(members) * GROUP
        here, rows = slice(0, count), slice(members[0] * GROUP, members[0] * GROUP + count)
        for g in members:
            resid_trips[g].arrive()
            by_group(g, norm_time)
        project_rows(normed_time, rows, w_temporal_qkv, packed_time, here)
        spread_heads(packed_time, heads_time, 3 * HEADS, here)

        def body(h, _):
            inner = pl.ds(pl.multiple_of(h * HEAD_DIM, 8), HEAD_DIM)
            for i, g in enumerate(members):
                part, whole_rows = slice(i * GROUP, (i + 1) * GROUP), slice(g * GROUP, (g + 1) * GROUP)
                values = heads_time[2 * HEADS + h, part]
                grad_queries, grad_keys, grad_values, soft = head_back(
                    heads_time[h, part],
                    heads_time[HEADS + h, part],
                    values,
                    grad_heads[h, whole_rows],
                    bias[...],
                )
                inner_tall[inner, whole_rows] = matmul(values, soft, TN)
                out_heads[h, part] = grad_queries
                out_heads[HEADS + h, part] = grad_keys
                out_heads[2 * HEADS + h, part] = grad_values
            return 0

        lax.fori_loop(0, HEADS, body, 0, unroll=UNROLL)
        for i in range(3 * HEADS):
            packed_grads[rows, i * HEAD_DIM : (i + 1) * HEAD_DIM] = out_heads[i, here]
        upstream_of(packed_grads, rows, w_temporal_qkv, low, count)

        for i, g in enumerate(members):

            def pull(g, start, _, i=i):
                grad = upstream_rows(low, i * GROUP + start, STEP)
                total = masked_rows(g, start) + norm_pullback(
                    frames(resid_place, g, start), grad, 1.0 + mod[4]
                )
                cot_blocks[g, pl.ds(lax.div(start, SPAN), STEP // SPAN)] = total.reshape(
                    STEP // SPAN, SPAN, D
                ).astype(HALF16)

            by_group(g, pull)
            grad_trips[g].start()

    temporal((0,))
    temporal((1, 2))
    transposed(normed_time, SPREAD, tall)
    weight_blocks(SPREAD, tall, packed_grads, inner_tall, scaled, low, high, grads_time)
    one.start()

    for g in range(GROUPS):
        grad_trips[g].arrive()
    for g in range(2):
        flat[g * GROUP : (g + 1) * GROUP, :] = wide(grad_place[g]).reshape(GROUP, D)
    for i in range(BLOCKS):
        start = 2 * GROUP + i * ODD
        flat[start : start + ODD, :] = wide(grad_place[2, i])[0:ODD]

    def scale(rows):
        scaled[rows, :] = (mod[2] * flat[rows, :]).astype(HALF16)

    by_rows(scale)
    every = slice(0, ROWS)
    grad_inner[every, :] = matmul(scaled[every, :], w_spatial_out[...], NT).astype(HALF16)
    spread_heads(grad_inner, grad_heads, HEADS, every)
    one.first()
    one.second()

    def attend_back(h, _):
        grad_queries, grad_keys, grad_values, _ = head_back(
            heads[h], heads[HEADS + h], heads[2 * HEADS + h], grad_heads[h, every]
        )
        out_heads[h] = grad_queries
        out_heads[HEADS + h] = grad_keys
        out_heads[2 * HEADS + h] = grad_values
        return 0

    lax.fori_loop(0, 4, attend_back, 0, unroll=UNROLL)
    one.third()
    lax.fori_loop(4, HEADS, attend_back, 0, unroll=UNROLL)
    one.fourth()
    for i in range(3 * HEADS):
        packed_grads[every, i * HEAD_DIM : (i + 1) * HEAD_DIM] = out_heads[i]
    transposed(normed, ROWS, tall)
    inner_tall[:, every] = wide(mixed[...]).T
    one.fifth()
    weight_blocks(ROWS, tall, packed_grads, inner_tall, scaled, low, high, grads_space)
    two.start()
    one.sixth(final_time, 0)
    one_z.start()
    two.first()
    two.second()
    upstream_of(packed_grads, every, w_spatial_qkv, low, ROWS)

    def last(start):
        rows = pl.ds(pl.multiple_of(start, STEP), STEP)
        grad = upstream_rows(low, start, STEP)
        grad_tokens[rows, :] = (
            flat[rows, :] + norm_pullback(wide(tokens[rows, :]), grad, 1.0 + mod[1])
        ).astype(HALF16)

    pl.loop(0, ROWS, step=STEP)(last)
    one_z.middle()
    two.third()
    two.fourth()
    one_z.end()
    two.fifth()
    two.sixth(final_space, 0)
    two_z.start()
    two_z.middle()
    two_z.end()
    for user in resid_trips + grad_trips + [one, two, one_z, two_z]:
        user.settle()


def vmem(shape, dtype=HALF16):
    return pltpu.VMEM(shape, dtype)


def run(lengths, mod, tokens, cotangent, w_spatial_qkv, w_spatial_out, w_temporal_qkv, w_temporal_out):
    full = jnp.float32
    place = vmem((GROUPS, BLOCKS, SPAN, D))
    scratch = [
        vmem((ROWS, D)),
        vmem((ROWS, D)),
        vmem((QKV, D)),
        vmem((INNER, D)),
        vmem((QKV, D)),
        vmem((INNER, D)),
        pltpu.SemaphoreType.DMA((6,)),
        place,
        place,
        place,
        place,
        place,
        vmem((ROWS, D), full),
        vmem((ROWS, D)),
        vmem((ROWS, QKV)),
        vmem((3 * HEADS, ROWS, HEAD_DIM)),
        vmem((HEADS, ROWS, HEAD_DIM)),
        vmem((ROWS, INNER)),
        vmem((SPREAD, D)),
        vmem((2 * GROUP, QKV)),
        vmem((3 * HEADS, 2 * GROUP, HEAD_DIM)),
        vmem((SPREAD, D)),
        vmem((SPREAD, INNER)),
        vmem((HEADS, SPREAD, HEAD_DIM)),
        vmem((3 * HEADS, ROWS, HEAD_DIM)),
        vmem((SPREAD, QKV)),
        vmem((INNER, SPREAD), full),
        vmem((D, SPREAD)),
        vmem((D, SPREAD), full),
        vmem((D, SPREAD), full),
        vmem((GROUP, GROUP), full),
        vmem((BLOCKS, 72, WIDE)),
        vmem((BLOCKS, 72, WIDE)),
        vmem((72, HALF)),
        vmem((72, HALF)),
    ]
    for _ in range(3 * GROUPS):
        scratch += exchange_sems()
    for _ in range(2):
        scratch += reduction_buffers() + reduction_sems()
    for _ in range(2):
        scratch += depth_buffers() + depth_sems()
    return pl.pallas_call(
        kernel,
        out_shape=(
            jax.ShapeDtypeStruct((ROWS, D), HALF16),
            jax.ShapeDtypeStruct((2, 72, WIDE), HALF16),
        ),
        in_specs=[pl.BlockSpec(memory_space=pltpu.SMEM), pl.BlockSpec(memory_space=pltpu.VMEM)]
        + [pl.BlockSpec(memory_space=pl.ANY)] * 6,
        out_specs=(pl.BlockSpec(memory_space=pltpu.VMEM), pl.BlockSpec(memory_space=pltpu.VMEM)),
        scratch_shapes=scratch,
        compiler_params=pltpu.CompilerParams(
            collective_id=0, has_side_effects=True, vmem_limit_bytes=VMEM_LIMIT
        ),
    )(lengths, mod, tokens, cotangent, w_spatial_qkv, w_spatial_out, w_temporal_qkv, w_temporal_out)


def unpack_grads(summed, item):
    left, right = (half[:, item * HALF : (item + 1) * HALF] for half in (summed[0], summed[1]))
    tall = right[:, QKV - HALF :]
    return (
        jnp.concatenate([left, right[:, : QKV - HALF]], axis=-1),
        jnp.concatenate([tall[:36], tall[36:]], axis=-1),
    )


def local(
    tokens,
    cotangent,
    modulation,
    lengths,
    w_spatial_qkv,
    w_spatial_out,
    w_temporal_qkv,
    w_temporal_out,
):
    grad_tokens, summed = run(
        lengths,
        modulation.reshape(6, 1, D),
        tokens.reshape(ROWS, D),
        cotangent.reshape(ROWS, D),
        w_spatial_qkv.T,
        w_spatial_out,
        w_temporal_qkv.T,
        w_temporal_out,
    )
    temporal_qkv, temporal_out = unpack_grads(summed, 0)
    spatial_qkv, spatial_out = unpack_grads(summed, 1)
    return (
        grad_tokens.reshape(tokens.shape),
        spatial_qkv,
        spatial_out,
        temporal_qkv,
        temporal_out,
    )


def solution(mesh):
    placed = (
        P("dp", "seq", None, None),
        P("dp", "seq", None, None),
        P("dp", None, None),
        P("dp"),
        P(),
        P(),
        P(),
        P(),
    )
    return jax.shard_map(
        local,
        mesh=mesh,
        in_specs=placed,
        out_specs=(
            P("dp", "seq", None, None),
            P("seq", None),
            P("seq", None),
            P("seq", None),
            P("seq", None),
        ),
        check_vma=False,
    )
```

time: 165 us -> 130 us (0.79)
  Pallas kernels: 159 us -> 125 us
    pallas_call x3 -> x1, Pallas kernels: 159 us -> 125 us  [run(): pl.pallas_call(kernel, out_shape=(jax.ShapeDtypeStruct((ROWS, D), HALF16)...]
where the time goes in v3:
time: 130 us
  Pallas kernels  125 us (96%)
  local copies, waits for them, and re-layouts  2.23 us (2%)
  other arithmetic  1.59 us (1%)
  between operations  1.32 us (1%)
    pallas_call x1, Pallas kernels, run(): pl.pallas_call(kernel, out_shape=(jax.ShapeDtypeStruct((ROWS, D), HALF16)...  125 us

profile of v3, /device:TPU:1, one launch (start us, length us, event | category | flops | bytes accessed | tf_op | source)
XLA Modules:
  0.0 129.8 jit_solution(15064015204369785697)
XLA Ops:
  1.3 124.7 %shard_map.119 = (bf16[320,1152]{1,0:T(8,128)(2,1)}, bf16[2,72,2304]{2,1,0:T(8,128)(2,1)}) custom-call(s32[1]{0:T(128)S(6)} %copy.14.lengths, f32[6,1,1152]{2,1,0:T(1,128)} %bitcast.15, bf16[320,1152]{1,0:T(8,128)(2,1)} %bitcast.12, bf16[320,1152]{1,0:T(8,128)(2,1)} %bitcast.13, bf16[1728,1152]{1,0:T(8,128)(2,1)} %bitcast.10, ...), custom_call_target="tpu_custom_call" | custom-call | tf_op jit(solution)/shard_map/pallas_call | solution.py:961
  125.9 0.0 copy-start
  125.9 1.2 slice_bitcast_fusion.1
  127.2 0.1 fusion
  127.3 0.8 pad_maximum_fusion.2
  128.1 0.8 pad_maximum_fusion
  128.9 0.0 copy-done
  128.9 0.9 copy.15
  (2 shorter events, 0.0 us)
Async XLA Ops:
  125.9 3.0 %copy-start = (bf16[320,1152]{1,0:T(8,128)(2,1)S(1)}, bf16[320,1152]{1,0:T(8,128)(2,1)}, u32[]{:S(2)}) copy-start(bf16[320,1152]{1,0:T(8,128)(2,1)} %get-tuple-element.7) | copy-start | bytes 2211844
